TPU v7x, 256 devices: a whole 4x4x8 slice. The times are simulated.
256 devices in a mesh: case: 4 (over y), se: 64 (over x, z, core).
Axes of the slice: x: 4, y: 4, z: 8, core: 2. Of those that a mesh axis runs over, the one named last changes fastest.
Arguments:
- panel_press: bfloat16 [131072, 512], P('se', 'case'), may hold values from -1.5 to 1.5
- panel_owner: int32 [131072, 1], P('se'), may hold values from 0 to 63; in each aligned block of 2048 rows (0 to 2047, 2048 to 4095, ...) at most 64 rows name the same one
- panel_slot: int32 [131072], P('se'), may hold values from 0 to 511
- elem_count: int32 [64], P('se'), may hold values from 1024 to 4096
- flexibility: bfloat16 [64, 2560, 512], P('se'), may hold values from -0.25 to 0.25
- stress_matrix: bfloat16 [64, 4096, 2560], P('se', 'case'), may hold values from -0.125 to 0.125
- combination: bfloat16 [512, 256], replicated, may hold values from -0.25 to 0.25
Outputs:
- combined: bfloat16 [64, 4096, 256], P('se', 'case')
Inputs may be any that keep to these rules, and one draw needn't show every extreme that they name: `panel_owner`: of the 2048 panels of one index of se, at most 64 name one superelement, a bound that some block reaches of them.
All inputs are finite; a program needn't handle non-finite values.
Results may differ from a plain program's by a relative error of at most 0.0064.
Values may be sent and summed in bfloat16 or wider, within the bound.
No kernel may reach another device: no remote copies, remote signals or barrier semaphores. Data moves between devices by JAX's collectives and lax.ppermute only.
A program may use at most 128 MiB of HBM per device.

v0:
```python
import jax
import jax.numpy as jnp
from jax import lax
from jax.sharding import PartitionSpec as P


def per_device(
    panel_press, panel_owner, panel_slot, elem_count, flexibility, stress_matrix, combination
):
    owners = lax.axis_size("se")
    load_points = flexibility.shape[2]
    owner_ids = panel_owner[:, 0]
    segment_ids = owner_ids * load_points + panel_slot
    load_sums = jax.ops.segment_sum(
        panel_press.astype(jnp.float32), segment_ids, num_segments=owners * load_points
    )
    loads = lax.psum_scatter(load_sums, "se", scatter_dimension=0, tiled=True)
    displacement = jnp.dot(
        flexibility[0], loads.astype(jnp.bfloat16), preferred_element_type=jnp.float32
    ).astype(jnp.bfloat16)
    live_rows = elem_count[0]
    local_rows = stress_matrix.shape[1]
    case_index = lax.axis_index("case")
    stress_full = jnp.dot(
        stress_matrix[0],
        lax.all_gather(displacement, "case", axis=1, tiled=True),
        preferred_element_type=jnp.float32,
    )
    row_ids = case_index * local_rows + jnp.arange(local_rows, dtype=jnp.int32)
    stress = jnp.where(row_ids[:, None] < live_rows, stress_full, 0.0).astype(jnp.bfloat16)
    combined = jnp.dot(stress, combination, preferred_element_type=jnp.float32).astype(jnp.bfloat16)
    return combined[None]


def solution(mesh):
    return jax.shard_map(
        per_device,
        mesh=mesh,
        in_specs=(
            P("se", "case"),
            P("se", None),
            P("se"),
            P("se"),
            P("se", None, None),
            P("se", "case", None),
            P(),
        ),
        out_specs=P("se", "case", None),
        check_vma=False,
    )
```

profile of v0, /device:TPU:32, one launch (start us, length us, event | category | flops | bytes accessed | tf_op | source)
XLA Modules:
  0.0 272.1 jit_solution(4466822512089919945)
XLA Ops:
  6.5 0.0 copy-start
  6.5 0.0 reduce-scatter.2.cloned.1.call-start
  6.5 0.9 broadcast_multiply_fusion
  7.4 0.7 add.19
  8.1 18.6 %scatter_custom_fusion = f32[32768,128]{1,0:T(8,128)} fusion(s32[2048]{0:T(1024)S(1)} %add.19, f32[]{:T(128)} %constant.4.clone.1, bf16[2048,128]{1,0:T(8,128)(2,1)} %param.7), kind=kCustom, calls=%fused_computation.1 | custom fusion | flops 524288 | bytes 17301508 | tf_op jit(solution)/shard_map/scatter-add | solution.py:14
  26.7 0.0 reduce-scatter.2.cloned.1.call-update
  26.7 0.0 copy-start.1
  26.7 0.0 all-gather.2.cloned.1.call-start
  26.8 191.2 %reduce-scatter.2.cloned.1.call-done = f32[512,128]{1,0:T(8,128)} async-done(((f32[32768,128]{1,0:T(8,128)}), f32[512,128]{1,0:T(8,128)}) %reduce-scatter.2.cloned.1.call-update) | async-done | bytes 262160 | tf_op jit(solution)/shard_map/reduce_scatter | solution.py:17
  218.0 0.0 copy-done
  218.0 2.8 %fusion.4 = bf16[2560,128]{0,1:T(8,128)(2,1)} fusion(bf16[1,2560,512]{2,1,0:T(8,128)(2,1)S(1)} %copy-done, f32[512,128]{1,0:T(8,128)} %reduce-scatter.2.cloned.1.call-done), kind=kOutput, calls=%fused_computation.6 | convolution fusion | flops 335937536 | bytes 3538944 | tf_op jit(solution)/shard_map/dot_general | solution.py:18
  220.8 0.0 all-gather.2.cloned.1.call-update
  221.5 36.4 %all-gather.2.cloned.1.call-done = bf16[2560,512]{0,1:T(8,128)(2,1)} async-done(((bf16[2560,128]{0,1:T(8,128)(2,1)}), bf16[2560,512]{0,1:T(8,128)(2,1)}) %all-gather.2.cloned.1.call-update) | async-done | bytes 2621456 | tf_op jit(solution)/shard_map/all_gather | solution.py:26
  257.9 0.0 copy-done.1
  257.9 7.3 %fusion.8 = bf16[1,1024,256]{2,1,0:T(8,128)(2,1)} fusion(bf16[512,256]{1,0:T(8,128)(2,1)S(1)} %copy-done.1, bf16[2560,512]{0,1:T(8,128)(2,1)} %all-gather.2.cloned.1.call-done, bf16[1,1024,2560]{2,1,0:T(8,128)(2,1)} %param.12, pred[1024]{0:T(1024)(128)(4,1)S(1)} %add_compare_fusion), kind=kOutput, calls=%fused_computation.10 | convolution fusion | flops 2954100736 | bytes 8651776 | tf_op jit(solution)/shard_map/dot_general | solution.py:31
  (1 shorter events, 0.0 us)
Async XLA Ops:
  6.5 211.5 %copy-start = (bf16[1,2560,512]{2,1,0:T(8,128)(2,1)S(1)}, bf16[1,2560,512]{2,1,0:T(8,128)(2,1)}, u32[]{:S(2)}) copy-start(bf16[1,2560,512]{2,1,0:T(8,128)(2,1)} %param.11) | copy-start | bytes 7864324
  6.5 211.5 %reduce-scatter.2.cloned.1.call-start = ((), (), s32[]{:S(2)}) async-start(), calls=%async_computation.1 | async-start | bytes 17039360 | tf_op jit(solution)/shard_map/reduce_scatter | solution.py:17
  26.7 231.2 %copy-start.1 = (bf16[512,256]{1,0:T(8,128)(2,1)S(1)}, bf16[512,256]{1,0:T(8,128)(2,1)}, u32[]{:S(2)}) copy-start(bf16[512,256]{1,0:T(8,128)(2,1)} %param.13) | copy-start | bytes 786436
  26.7 231.2 %all-gather.2.cloned.1.call-start = ((), (), s32[]{:S(2)}) async-start(), calls=%async_computation.2 | async-start | bytes 3276800 | tf_op jit(solution)/shard_map/all_gather | solution.py:26
Sparse Core Ops, SparseCore 0:
  26.8 191.1 reduce-scatter.1
  221.0 36.9 all-gather.1
where the time goes:
time: 273 us; the launch traced here: 272 us
  waiting for transfers between devices  228 us (84%)
  other arithmetic  20.2 us (7%)
  between operations  14.1 us (5%)
  matrix products  10.1 us (4%)
    reduce_scatter x1, waiting for transfers between devices, per_device(): loads = lax.psum_scatter(load_sums, 'se', scatter_dimension=0, tiled=True)  191 us
    all_gather x1, waiting for transfers between devices, per_device(): lax.all_gather(displacement, 'case', axis=1, tiled=True)  36.4 us
    scatter-add x1, other arithmetic, per_device(): jax.ops.segment_sum(panel_press.astype(jnp.float32), segment_ids, num_seg...  18.6 us
    dot_general x1, matrix products, per_device(): jnp.dot(stress, combination, preferred_element_type=jnp.float32)  7.29 us
  transfers between devices with their start and end apart: 2, of which 2 were waited for; matrix products, arithmetic and copies ran while one was open for 0% of the time, Pallas kernels for 0%

commit v1 on v0

v1 whole, which is shorter than its diff:
```python
import jax
import jax.numpy as jnp
from jax import lax
from jax.experimental import pallas as pl
from jax.experimental.pallas import tpu as pltpu
from jax.sharding import PartitionSpec as P

NX, NZ, NC = 4, 8, 2
CAP = 64
NEAR = NX * NC
ROWS = NEAR * CAP
META = 16
MSG = ROWS + META
BF, F32 = jnp.bfloat16, jnp.float32


def iota(shape, dim):
    return lax.broadcasted_iota(jnp.int32, shape, dim)


def one_hot(mask):
    return jnp.where(mask, 1.0, 0.0).astype(BF)


def pack_kernel(owner_ref, slot_ref, press_ref, out_ref, place_ref, dist_ref, meta_ref):
    step = pl.program_id(0)
    panels = press_ref.shape[0]

    @pl.when(step == 0)
    def _():
        me = lax.axis_index("se")
        owner = owner_ref[...]
        dx = ((owner >> 4) - (me >> 4)) & (NX - 1)
        dz = ((owner >> 1) - (me >> 1)) & (NZ - 1)
        dc = (owner ^ me) & 1
        near = dc * NX + dx
        q = dz * NEAR + near
        oh_q = one_hot(iota((NZ * NEAR, panels), 0) == q)
        width = 256
        before = one_hot(iota((width, width), 0) < iota((width, width), 1))
        blocks = one_hot((iota((panels, 128), 0) // width) < iota((panels, 128), 1))
        starts = jnp.dot(oh_q, blocks, preferred_element_type=F32)
        ranks = []
        for b in range(panels // width):
            part = oh_q[:, b * width : (b + 1) * width]
            count = jnp.dot(part, before, preferred_element_type=F32) + starts[:, b : b + 1]
            ranks.append(jnp.sum(part.astype(F32) * count, axis=0, keepdims=True))
        rank = jnp.concatenate(ranks, axis=1).astype(jnp.int32)
        place_ref[...] = one_hot(iota((ROWS, panels), 0) == near * CAP + rank)
        dist_ref[...] = jnp.where(iota((NZ, panels), 0) == dz, 1.0, 0.0)
        row = iota((NZ * META, panels), 0)
        hit = ((row >> 4) == dz) & ((row & 15) == (near >> 1))
        value = (slot_ref[...] - 256).astype(F32)
        rows_at = jnp.where(hit, value, 0.0).astype(BF)
        lanes_at = one_hot(iota((128, panels), 0) == (near & 1) * CAP + rank)
        meta_ref[...] = lax.dot_general(
            rows_at, lanes_at, (((1,), (1,)), ((), ())), preferred_element_type=F32
        ).astype(BF)

    chosen = place_ref[...] * dist_ref[pl.ds(step, 1), :].astype(BF)
    out_ref[0, :ROWS, :] = jnp.dot(chosen, press_ref[...], preferred_element_type=F32).astype(BF)
    out_ref[0, ROWS:, :] = meta_ref[pl.ds(pl.multiple_of(step * META, META), META), :]


def pack(owner, slot, press):
    panels, cases = press.shape
    return pl.pallas_call(
        pack_kernel,
        grid=(NZ,),
        in_specs=[
            pl.BlockSpec((1, panels), lambda i: (0, 0)),
            pl.BlockSpec((1, panels), lambda i: (0, 0)),
            pl.BlockSpec((panels, cases), lambda i: (0, 0)),
        ],
        out_specs=pl.BlockSpec((1, MSG, cases), lambda i: (i, 0, 0)),
        out_shape=jax.ShapeDtypeStruct((NZ, MSG, cases), BF),
        scratch_shapes=[
            pltpu.VMEM((ROWS, panels), BF),
            pltpu.VMEM((NZ, panels), F32),
            pltpu.VMEM((NZ * META, 128), BF),
        ],
        compiler_params=pltpu.CompilerParams(vmem_limit_bytes=32 << 20),
        cost_estimate=pl.CostEstimate(
            flops=2 * NZ * ROWS * panels * cases, bytes_accessed=2 << 20, transcendentals=0
        ),
        name="pack",
    )(owner, slot, press)


def scatter_kernel(*refs):
    msgs, (own_ref, mate_ref) = refs[:NZ], refs[NZ:]
    points = own_ref.shape[1]
    lane = iota((1, 128), 1)
    point = iota((points, 128), 0)
    for near in range(NEAR):
        row = near // 2
        ohs, data = [], []
        for m in range(0, NZ, 2):
            first = msgs[m][ROWS : ROWS + META, :].astype(F32)[row : row + 1, :]
            second = msgs[m + 1][ROWS : ROWS + META, :].astype(F32)[row : row + 1, :]
            if near % 2 == 0:
                second = pltpu.roll(second, CAP, 1)
            else:
                first = pltpu.roll(first, CAP, 1)
            slots = jnp.where(lane < CAP, first, second).astype(jnp.int32) + 256
            ohs.append(one_hot(point == slots))
            data.append(msgs[m][near * CAP : (near + 1) * CAP, :])
            data.append(msgs[m + 1][near * CAP : (near + 1) * CAP, :])
        total = jnp.dot(
            jnp.concatenate(ohs, axis=1),
            jnp.concatenate(data, axis=0),
            preferred_element_type=F32,
        ).astype(BF)
        target = own_ref if near < NX else mate_ref
        target[near % NX] = total


def scatter(messages, points):
    cases = messages[0].shape[1]
    shape = jax.ShapeDtypeStruct((NX, points, cases), BF)
    return pl.pallas_call(
        scatter_kernel,
        out_shape=(shape, shape),
        compiler_params=pltpu.CompilerParams(vmem_limit_bytes=32 << 20),
        cost_estimate=pl.CostEstimate(
            flops=2 * NEAR * points * ROWS * cases, bytes_accessed=4 << 20, transcendentals=0
        ),
        name="scatter",
    )(*messages)


def finish_kernel(live_ref, *refs):
    loads, (comb_ref, mat_ref, out_ref) = refs[:NX], refs[NX:]
    y = lax.axis_index("case")
    cases = loads[0].shape[1]
    total = None
    for k in range(len(loads)):
        block = pl.multiple_of(((y - k) & 3) * cases, cases)
        term = jnp.dot(loads[k][...], comb_ref[pl.ds(block, cases), :], preferred_element_type=F32)
        total = term if total is None else total + term
    rows = out_ref.shape[0]
    out = jnp.dot(mat_ref[...], total.astype(BF), preferred_element_type=F32)
    live = y * rows + iota(out.shape, 0) < live_ref[0]
    out_ref[...] = jnp.where(live, out, 0.0).astype(BF)


def finish(live, loads, comb, mat):
    vmem = pl.BlockSpec(memory_space=pltpu.VMEM)
    return pl.pallas_call(
        finish_kernel,
        in_specs=[pl.BlockSpec(memory_space=pltpu.SMEM)] + [vmem] * (len(loads) + 2),
        out_specs=vmem,
        out_shape=jax.ShapeDtypeStruct((mat.shape[0], comb.shape[1]), BF),
        compiler_params=pltpu.CompilerParams(vmem_limit_bytes=32 << 20),
        cost_estimate=pl.CostEstimate(flops=400 << 20, bytes_accessed=3 << 20, transcendentals=0),
        name="finish",
    )(live, *loads, comb, mat)


def se_index(x, z, c):
    return ((x % NX) * NZ + z % NZ) * NC + c % NC


def moved(dx, dz, dc):
    return [
        (se_index(x, z, c), se_index(x + dx, z + dz, c + dc))
        for x in range(NX)
        for z in range(NZ)
        for c in range(NC)
    ]


def per_device(
    panel_press, panel_owner, panel_slot, elem_count, flexibility, stress_matrix, combination
):
    panels = panel_press.shape[0]
    points = flexibility.shape[2]
    packed = pack(
        panel_owner.reshape(1, panels), panel_slot.reshape(1, panels), panel_press
    )
    messages = [packed[0]] + [None] * (NZ - 1)
    for k in (4, 3, 5, 2, 6, 1, 7):
        messages[k] = lax.ppermute(packed[k], "se", moved(0, k, 0))
    mat = jnp.dot(
        stress_matrix[0], flexibility[0], preferred_element_type=F32
    ).astype(BF)
    own, mate = scatter(messages, points)
    mate = lax.ppermute(mate, "se", moved(0, 0, 1))
    sums = (own.astype(F32) + mate.astype(F32)).astype(BF)
    total = sums[0].astype(F32)
    for k in (2, 1, 3):
        total = total + lax.ppermute(sums[k], "se", moved(k, 0, 0)).astype(F32)
    loads = [total.astype(BF)] + [None] * (NX - 1)
    for k in (2, 1, 3):
        loads[k] = lax.ppermute(loads[0], "case", [(y, (y + k) % 4) for y in range(4)])
    return finish(elem_count, loads, combination, mat)[None]


def solution(mesh):
    return jax.shard_map(
        per_device,
        mesh=mesh,
        in_specs=(
            P("se", "case"),
            P("se", None),
            P("se"),
            P("se"),
            P("se", None, None),
            P("se", "case", None),
            P(),
        ),
        out_specs=P("se", "case", None),
        check_vma=False,
    )
```

time: 273 us -> 75.7 us (0.28)
  waiting for transfers between devices: 228 us -> 28.6 us
  starting transfers between devices: 0.04 us -> 29.5 us
  other arithmetic: 20.2 us -> 0.22 us
  between operations: 14.1 us -> 0.74 us
  Pallas kernels: 0 us -> 10.9 us
  matrix products: 10.1 us -> 2.86 us
    reduce_scatter x1 -> x0, waiting for transfers between devices: 191 us -> none  [per_device(): loads = lax.psum_scatter(load_sums, 'se', scatter_dimension=0, tiled=True)]
    all_gather x1 -> x0, waiting for transfers between devices: 36.4 us -> none  [per_device(): lax.all_gather(displacement, 'case', axis=1, tiled=True)]
    ppermute x0 -> x14, starting transfers between devices: none -> 29.5 us  [the longest x7 18.8 us: per_device(): messages[k] = lax.ppermute(packed[k], 'se', moved(0, k, 0))]
    ppermute x0 -> x14, waiting for transfers between devices: none -> 28.6 us  [the longest x7 17.4 us: per_device(): messages[k] = lax.ppermute(packed[k], 'se', moved(0, k, 0))]
    scatter-add x1 -> x0, other arithmetic: 18.6 us -> none  [per_device(): jax.ops.segment_sum(panel_press.astype(jnp.float32), segment_ids, num_seg...]
    pallas_call x0 -> x3, Pallas kernels: none -> 10.9 us  [the longest x1 7.58 us: pack(): pl.pallas_call(pack_kernel, grid=(NZ,), in_specs=[pl.BlockSpec((1, panels...]
    dot_general x2 -> x1, matrix products: 10.1 us -> 2.86 us  [per_device(): jnp.dot(stress_matrix[0], flexibility[0], preferred_element_type=F32)]
  transfers between devices with their start and end apart: 2 -> 14, of which waited for: 2 -> 9; matrix products, arithmetic and copies ran while one was open for 0% -> 4% of each run, Pallas kernels for 0% -> 0%
where the time goes in v1:
time: 75.7 us; the launch traced here: 75.5 us
  starting transfers between devices  29.5 us (39%)
  waiting for transfers between devices  28.6 us (38%)
  Pallas kernels  10.9 us (14%)
  matrix products  2.86 us (4%)
  local copies, waits for them, and re-layouts  2.7 us (4%)
    ppermute x7, starting transfers between devices, per_device(): messages[k] = lax.ppermute(packed[k], 'se', moved(0, k, 0))  18.8 us
    ppermute x7, waiting for transfers between devices, per_device(): messages[k] = lax.ppermute(packed[k], 'se', moved(0, k, 0))  17.4 us
    ppermute x3, waiting for transfers between devices, per_device(): total = total + lax.ppermute(sums[k], 'se', moved(k, 0, 0)).astype(F32)  7.9 us
    pallas_call x1, Pallas kernels, pack(): pl.pallas_call(pack_kernel, grid=(NZ,), in_specs=[pl.BlockSpec((1, panels...  7.58 us
    ppermute x3, starting transfers between devices, per_device(): lax.ppermute(loads[0], 'case', [(y, (y + k) % 4) for y in range(4)])  6.09 us
    ppermute x3, starting transfers between devices, per_device(): total = total + lax.ppermute(sums[k], 'se', moved(k, 0, 0)).astype(F32)  4.51 us
    dot_general x1, matrix products, per_device(): jnp.dot(stress_matrix[0], flexibility[0], preferred_element_type=F32)  2.86 us
    unnamed x12, local copies, waits for them, and re-layouts  2.6 us
  transfers between devices with their start and end apart: 14, of which 9 were waited for; matrix products, arithmetic and copies ran while one was open for 4% of the time, Pallas kernels for 0%

profile of v1, /device:TPU:32, one launch (start us, length us, event | category | flops | bytes accessed | tf_op | source)
XLA Modules:
  0.0 75.5 jit_solution(1701074558178740993)
XLA Ops:
  0.0 1.2 %copy-done.2 = bf16[2048,128]{1,0:T(8,128)(2,1)S(1)} copy-done((bf16[2048,128]{1,0:T(8,128)(2,1)S(1)}, bf16[2048,128]{1,0:T(8,128)(2,1)}, u32[]{:S(2)}) %copy-start.2) | copy-done | bytes 524312
  2.6 7.6 %pack.1 = bf16[8,528,128]{2,1,0:T(8,128)(2,1)S(1)} custom-call(s32[1,2048]{1,0:T(1,128)S(1)} %bitcast.40, s32[1,2048]{1,0:T(1,128)S(1)} %bitcast.41, bf16[2048,128]{1,0:T(8,128)(2,1)S(1)} %copy-done.2), custom_call_target="tpu_custom_call" | custom-call | flops 2147483648 | bytes 2097152 | tf_op jit(solution)/shard_map/pack/pallas_call | solution.py:67
  10.3 2.0 %collective-permute-start = (bf16[528,128]{1,0:T(8,128)(2,1)S(1)}, bf16[528,128]{1,0:T(8,128)(2,1)S(1)}, u32[]{:S(2)}, u32[]{:S(2)}) collective-permute-start(bf16[528,128]{1,0:T(8,128)(2,1)S(1)} %get-tuple-element.15), channel_id=1, source_target_pairs={{0,2},{1,3},{2,4},{3,5},{4,6},{5,7},{6,8},{7,9},{8,10},{9,11},{10,... | collective-permute-start | bytes 405512 | tf_op jit(solution)/shard_map/ppermute | solution.py:183
  12.3 4.5 %collective-permute-start.1 = (bf16[528,128]{1,0:T(8,128)(2,1)S(1)}, bf16[528,128]{1,0:T(8,128)(2,1)S(1)}, u32[]{:S(2)}, u32[]{:S(2)}) collective-permute-start(bf16[528,128]{1,0:T(8,128)(2,1)S(1)} %get-tuple-element.14), channel_id=1, source_target_pairs={{0,4},{1,5},{2,6},{3,7},{4,8},{5,9},{6,10},{7,11},{8,12},{9,13},{1... | collective-permute-start | bytes 405512 | tf_op jit(solution)/shard_map/ppermute | solution.py:183
  16.8 1.9 %collective-permute-start.2 = (bf16[528,128]{1,0:T(8,128)(2,1)S(1)}, bf16[528,128]{1,0:T(8,128)(2,1)S(1)}, u32[]{:S(2)}, u32[]{:S(2)}) collective-permute-start(bf16[528,128]{1,0:T(8,128)(2,1)S(1)} %get-tuple-element.13), channel_id=1, source_target_pairs={{0,6},{1,7},{2,8},{3,9},{4,10},{5,11},{6,12},{7,13},{8,14},{9,15},... | collective-permute-start | bytes 405512 | tf_op jit(solution)/shard_map/ppermute | solution.py:183
  18.7 1.4 %collective-permute-start.3 = (bf16[528,128]{1,0:T(8,128)(2,1)S(1)}, bf16[528,128]{1,0:T(8,128)(2,1)S(1)}, u32[]{:S(2)}, u32[]{:S(2)}) collective-permute-start(bf16[528,128]{1,0:T(8,128)(2,1)S(1)} %get-tuple-element.12), channel_id=1, source_target_pairs={{0,8},{1,9},{2,10},{3,11},{4,12},{5,13},{6,14},{7,15},{8,0},{9,1},... | collective-permute-start | bytes 405512 | tf_op jit(solution)/shard_map/ppermute | solution.py:183
  20.1 3.1 %collective-permute-start.4 = (bf16[528,128]{1,0:T(8,128)(2,1)S(1)}, bf16[528,128]{1,0:T(8,128)(2,1)S(1)}, u32[]{:S(2)}, u32[]{:S(2)}) collective-permute-start(bf16[528,128]{1,0:T(8,128)(2,1)S(1)} %get-tuple-element.11), channel_id=1, source_target_pairs={{0,10},{1,11},{2,12},{3,13},{4,14},{5,15},{6,0},{7,1},{8,2},{9,3},... | collective-permute-start | bytes 405512 | tf_op jit(solution)/shard_map/ppermute | solution.py:183
  23.2 2.4 %collective-permute-start.5 = (bf16[528,128]{1,0:T(8,128)(2,1)S(1)}, bf16[528,128]{1,0:T(8,128)(2,1)S(1)}, u32[]{:S(2)}, u32[]{:S(2)}) collective-permute-start(bf16[528,128]{1,0:T(8,128)(2,1)S(1)} %get-tuple-element.10), channel_id=1, source_target_pairs={{0,12},{1,13},{2,14},{3,15},{4,0},{5,1},{6,2},{7,3},{8,4},{9,5},{1... | collective-permute-start | bytes 405512 | tf_op jit(solution)/shard_map/ppermute | solution.py:183
  26.1 3.4 %collective-permute-start.6 = (bf16[528,128]{1,0:T(8,128)(2,1)S(1)}, bf16[528,128]{1,0:T(8,128)(2,1)S(1)}, u32[]{:S(2)}, u32[]{:S(2)}) collective-permute-start(bf16[528,128]{1,0:T(8,128)(2,1)S(1)} %get-tuple-element.9), channel_id=1, source_target_pairs={{0,14},{1,15},{2,0},{3,1},{4,2},{5,3},{6,4},{7,5},{8,6},{9,7},{10,... | collective-permute-start | bytes 405512 | tf_op jit(solution)/shard_map/ppermute | solution.py:183
  29.5 9.6 %collective-permute-done.2.refs_3_ = bf16[528,128]{1,0:T(8,128)(2,1)S(1)} collective-permute-done((bf16[528,128]{1,0:T(8,128)(2,1)S(1)}, bf16[528,128]{1,0:T(8,128)(2,1)S(1)}, u32[]{:S(2)}, u32[]{:S(2)}) %collective-permute-start.2) | collective-permute-done | bytes 135200 | tf_op jit(solution)/shard_map/ppermute | solution.py:183
  39.0 6.0 %collective-permute-done.5.refs_6_ = bf16[528,128]{1,0:T(8,128)(2,1)S(1)} collective-permute-done((bf16[528,128]{1,0:T(8,128)(2,1)S(1)}, bf16[528,128]{1,0:T(8,128)(2,1)S(1)}, u32[]{:S(2)}, u32[]{:S(2)}) %collective-permute-start.5) | collective-permute-done | bytes 135200 | tf_op jit(solution)/shard_map/ppermute | solution.py:183
  45.0 1.4 %collective-permute-done.6.refs_7_ = bf16[528,128]{1,0:T(8,128)(2,1)S(1)} collective-permute-done((bf16[528,128]{1,0:T(8,128)(2,1)S(1)}, bf16[528,128]{1,0:T(8,128)(2,1)S(1)}, u32[]{:S(2)}, u32[]{:S(2)}) %collective-permute-start.6) | collective-permute-done | bytes 135200 | tf_op jit(solution)/shard_map/ppermute | solution.py:183
  46.5 1.3 %scatter.1 = (bf16[4,512,128]{2,1,0:T(8,128)(2,1)S(1)}, bf16[4,512,128]{2,1,0:T(8,128)(2,1)S(1)}) custom-call(bf16[528,128]{1,0:T(8,128)(2,1)S(1)} %get-tuple-element.16.refs_0_, bf16[528,128]{1,0:T(8,128)(2,1)S(1)} %collective-permute-done.refs_1_, bf16[528,128]{1,0:T(8,128)(2,1)S(1)} %collective-permute-done.1.refs_2_, ...), custom_call_target="tpu_custom_call" | custom-call | flops 536870912 | bytes 4194304 | tf_op jit(solution)/shard_map/scatter/pallas_call | solution.py:121
  47.9 1.9 %collective-permute-done.7 = bf16[4,512,128]{2,1,0:T(8,128)(2,1)S(1)} collective-permute-done((bf16[4,512,128]{2,1,0:T(8,128)(2,1)S(1)}, bf16[4,512,128]{2,1,0:T(8,128)(2,1)S(1)}, u32[]{:S(2)}, u32[]{:S(2)}) %collective-permute-start.7) | collective-permute-done | bytes 524320 | tf_op jit(solution)/shard_map/ppermute | solution.py:188
  50.0 2.8 %collective-permute-start.10 = (bf16[512,128]{1,0:T(8,128)(2,1)S(1)}, bf16[512,128]{1,0:T(8,128)(2,1)S(1)}, u32[]{:S(2)}, u32[]{:S(2)}) collective-permute-start(bf16[512,128]{1,0:T(8,128)(2,1)S(1)} %get-tuple-element.18), channel_id=1, source_target_pairs={{0,48},{1,49},{2,50},{3,51},{4,52},{5,53},{6,54},{7,55},{8,56},{9,... | collective-permute-start | bytes 393224 | tf_op jit(solution)/shard_map/ppermute | solution.py:192
  54.5 4.2 %collective-permute-done.10 = bf16[512,128]{1,0:T(8,128)(2,1)S(1)} collective-permute-done((bf16[512,128]{1,0:T(8,128)(2,1)S(1)}, bf16[512,128]{1,0:T(8,128)(2,1)S(1)}, u32[]{:S(2)}, u32[]{:S(2)}) %collective-permute-start.10) | collective-permute-done | bytes 131104 | tf_op jit(solution)/shard_map/ppermute | solution.py:192
  58.7 2.0 %collective-permute-done.8 = bf16[512,128]{1,0:T(8,128)(2,1)S(1)} collective-permute-done((bf16[512,128]{1,0:T(8,128)(2,1)S(1)}, bf16[512,128]{1,0:T(8,128)(2,1)S(1)}, u32[]{:S(2)}, u32[]{:S(2)}) %collective-permute-start.8) | collective-permute-done | bytes 131104 | tf_op jit(solution)/shard_map/ppermute | solution.py:192
  60.7 1.7 %collective-permute-done.9 = bf16[512,128]{1,0:T(8,128)(2,1)S(1)} collective-permute-done((bf16[512,128]{1,0:T(8,128)(2,1)S(1)}, bf16[512,128]{1,0:T(8,128)(2,1)S(1)}, u32[]{:S(2)}, u32[]{:S(2)}) %collective-permute-start.9) | collective-permute-done | bytes 131104 | tf_op jit(solution)/shard_map/ppermute | solution.py:192
  62.5 1.8 %collective-permute-start.11 = (bf16[512,128]{1,0:T(8,128)(2,1)S(1)}, bf16[512,128]{1,0:T(8,128)(2,1)S(1)}, u32[]{:S(2)}, u32[]{:S(2)}) collective-permute-start(bf16[512,128]{1,0:T(8,128)(2,1)S(1)} %fusion.10.refs_0_), channel_id=1, source_target_pairs={{0,64},{64,128},{128,192},{192,0},{1,65},{65,129},{129,193},{193,1... | collective-permute-start | bytes 393224 | tf_op jit(solution)/shard_map/ppermute | solution.py:195
  64.3 2.9 %collective-permute-start.12 = (bf16[512,128]{1,0:T(8,128)(2,1)S(1)}, bf16[512,128]{1,0:T(8,128)(2,1)S(1)}, u32[]{:S(2)}, u32[]{:S(2)}) collective-permute-start(bf16[512,128]{1,0:T(8,128)(2,1)S(1)} %fusion.10.refs_0_), channel_id=1, source_target_pairs={{0,128},{64,192},{128,0},{192,64},{1,129},{65,193},{129,1},{193,65... | collective-permute-start | bytes 393224 | tf_op jit(solution)/shard_map/ppermute | solution.py:195
  67.2 1.3 %collective-permute-start.13 = (bf16[512,128]{1,0:T(8,128)(2,1)S(1)}, bf16[512,128]{1,0:T(8,128)(2,1)S(1)}, u32[]{:S(2)}, u32[]{:S(2)}) collective-permute-start(bf16[512,128]{1,0:T(8,128)(2,1)S(1)} %fusion.10.refs_0_), channel_id=1, source_target_pairs={{0,192},{64,0},{128,64},{192,128},{1,193},{65,1},{129,65},{193,129... | collective-permute-start | bytes 393224 | tf_op jit(solution)/shard_map/ppermute | solution.py:195
  68.6 2.9 %fusion.3.refs_5_ = bf16[1024,512]{1,0:T(8,128)(2,1)S(1)} fusion(bf16[1,2560,512]{2,1,0:T(8,128)(2,1)S(1)} %copy-done, bf16[1,1024,2560]{2,1,0:T(8,128)(2,1)S(1)} %copy-done.5), kind=kOutput, calls=%fused_computation.3 | convolution fusion | flops 2684878848 | bytes 8912896 | tf_op jit(solution)/shard_map/dot_general | solution.py:184
  72.1 1.3 %collective-permute-done.12.refs_2_ = bf16[512,128]{1,0:T(8,128)(2,1)S(1)} collective-permute-done((bf16[512,128]{1,0:T(8,128)(2,1)S(1)}, bf16[512,128]{1,0:T(8,128)(2,1)S(1)}, u32[]{:S(2)}, u32[]{:S(2)}) %collective-permute-start.12) | collective-permute-done | bytes 131104 | tf_op jit(solution)/shard_map/ppermute | solution.py:195
  73.4 2.1 %finish.1 = bf16[1024,256]{1,0:T(8,128)(2,1)} custom-call(s32[1]{0:T(128)S(6)} %copy.8.live_ref, bf16[512,128]{1,0:T(8,128)(2,1)S(1)} %fusion.10.refs_0_, bf16[512,128]{1,0:T(8,128)(2,1)S(1)} %collective-permute-done.11.refs_1_, bf16[512,128]{1,0:T(8,128)(2,1)S(1)} %collective-permute-done.12.refs_2_, bf16[512,128]{1,0:T(8,128)(2,1)S(1)} %collective-permute-done.13.refs_3_, ...), custom_call_target="tpu_custom_call" | custom-call | flops 419430400 | bytes 3145728 | tf_op jit(solution)/shard_map/finish/pallas_call | solution.py:149
  (24 shorter events, 4.0 us)
Async XLA Ops:
  0.0 68.6 %copy-start = (bf16[1,2560,512]{2,1,0:T(8,128)(2,1)S(1)}, bf16[1,2560,512]{2,1,0:T(8,128)(2,1)}, u32[]{:S(2)}) copy-start(bf16[1,2560,512]{2,1,0:T(8,128)(2,1)} %param.11) | copy-start | bytes 7864324
  0.0 1.2 %copy-start.2 = (bf16[2048,128]{1,0:T(8,128)(2,1)S(1)}, bf16[2048,128]{1,0:T(8,128)(2,1)}, u32[]{:S(2)}) copy-start(bf16[2048,128]{1,0:T(8,128)(2,1)} %press_ref.1) | copy-start | bytes 1572868
  1.2 0.7 copy-start.3
  1.9 0.7 copy-start.4
  10.2 58.4 %copy-start.5 = (bf16[1,1024,2560]{2,1,0:T(8,128)(2,1)S(1)}, bf16[1,1024,2560]{2,1,0:T(8,128)(2,1)}, u32[]{:S(2)}) copy-start(bf16[1,1024,2560]{2,1,0:T(8,128)(2,1)} %param.12) | copy-start | bytes 15728644
  10.3 13.0 %collective-permute-start = (bf16[528,128]{1,0:T(8,128)(2,1)S(1)}, bf16[528,128]{1,0:T(8,128)(2,1)S(1)}, u32[]{:S(2)}, u32[]{:S(2)}) collective-permute-start(bf16[528,128]{1,0:T(8,128)(2,1)S(1)} %get-tuple-element.15), channel_id=1, source_target_pairs={{0,2},{1,3},{2,4},{3,5},{4,6},{5,7},{6,8},{7,9},{8,10},{9,11},{10,... | collective-permute-start | bytes 405512 | tf_op jit(solution)/shard_map/ppermute | solution.py:183
  12.3 13.8 %collective-permute-start.1 = (bf16[528,128]{1,0:T(8,128)(2,1)S(1)}, bf16[528,128]{1,0:T(8,128)(2,1)S(1)}, u32[]{:S(2)}, u32[]{:S(2)}) collective-permute-start(bf16[528,128]{1,0:T(8,128)(2,1)S(1)} %get-tuple-element.14), channel_id=1, source_target_pairs={{0,4},{1,5},{2,6},{3,7},{4,8},{5,9},{6,10},{7,11},{8,12},{9,13},{1... | collective-permute-start | bytes 405512 | tf_op jit(solution)/shard_map/ppermute | solution.py:183
  16.8 22.3 %collective-permute-start.2 = (bf16[528,128]{1,0:T(8,128)(2,1)S(1)}, bf16[528,128]{1,0:T(8,128)(2,1)S(1)}, u32[]{:S(2)}, u32[]{:S(2)}) collective-permute-start(bf16[528,128]{1,0:T(8,128)(2,1)S(1)} %get-tuple-element.13), channel_id=1, source_target_pairs={{0,6},{1,7},{2,8},{3,9},{4,10},{5,11},{6,12},{7,13},{8,14},{9,15},... | collective-permute-start | bytes 405512 | tf_op jit(solution)/shard_map/ppermute | solution.py:183
  18.7 20.4 %collective-permute-start.3 = (bf16[528,128]{1,0:T(8,128)(2,1)S(1)}, bf16[528,128]{1,0:T(8,128)(2,1)S(1)}, u32[]{:S(2)}, u32[]{:S(2)}) collective-permute-start(bf16[528,128]{1,0:T(8,128)(2,1)S(1)} %get-tuple-element.12), channel_id=1, source_target_pairs={{0,8},{1,9},{2,10},{3,11},{4,12},{5,13},{6,14},{7,15},{8,0},{9,1},... | collective-permute-start | bytes 405512 | tf_op jit(solution)/shard_map/ppermute | solution.py:183
  20.1 18.9 %collective-permute-start.4 = (bf16[528,128]{1,0:T(8,128)(2,1)S(1)}, bf16[528,128]{1,0:T(8,128)(2,1)S(1)}, u32[]{:S(2)}, u32[]{:S(2)}) collective-permute-start(bf16[528,128]{1,0:T(8,128)(2,1)S(1)} %get-tuple-element.11), channel_id=1, source_target_pairs={{0,10},{1,11},{2,12},{3,13},{4,14},{5,15},{6,0},{7,1},{8,2},{9,3},... | collective-permute-start | bytes 405512 | tf_op jit(solution)/shard_map/ppermute | solution.py:183
  23.2 21.8 %collective-permute-start.5 = (bf16[528,128]{1,0:T(8,128)(2,1)S(1)}, bf16[528,128]{1,0:T(8,128)(2,1)S(1)}, u32[]{:S(2)}, u32[]{:S(2)}) collective-permute-start(bf16[528,128]{1,0:T(8,128)(2,1)S(1)} %get-tuple-element.10), channel_id=1, source_target_pairs={{0,12},{1,13},{2,14},{3,15},{4,0},{5,1},{6,2},{7,3},{8,4},{9,5},{1... | collective-permute-start | bytes 405512 | tf_op jit(solution)/shard_map/ppermute | solution.py:183
  26.1 20.4 %collective-permute-start.6 = (bf16[528,128]{1,0:T(8,128)(2,1)S(1)}, bf16[528,128]{1,0:T(8,128)(2,1)S(1)}, u32[]{:S(2)}, u32[]{:S(2)}) collective-permute-start(bf16[528,128]{1,0:T(8,128)(2,1)S(1)} %get-tuple-element.9), channel_id=1, source_target_pairs={{0,14},{1,15},{2,0},{3,1},{4,2},{5,3},{6,4},{7,5},{8,6},{9,7},{10,... | collective-permute-start | bytes 405512 | tf_op jit(solution)/shard_map/ppermute | solution.py:183
  47.8 2.0 %collective-permute-start.7 = (bf16[4,512,128]{2,1,0:T(8,128)(2,1)S(1)}, bf16[4,512,128]{2,1,0:T(8,128)(2,1)S(1)}, u32[]{:S(2)}, u32[]{:S(2)}) collective-permute-start(bf16[4,512,128]{2,1,0:T(8,128)(2,1)S(1)} %get-tuple-element.8), channel_id=1, source_target_pairs={{0,1},{1,0},{2,3},{3,2},{4,5},{5,4},{6,7},{7,6},{8,9},{9,8},{10,11... | collective-permute-start | bytes 1572872 | tf_op jit(solution)/shard_map/ppermute | solution.py:188
  50.0 8.7 %collective-permute-start.10 = (bf16[512,128]{1,0:T(8,128)(2,1)S(1)}, bf16[512,128]{1,0:T(8,128)(2,1)S(1)}, u32[]{:S(2)}, u32[]{:S(2)}) collective-permute-start(bf16[512,128]{1,0:T(8,128)(2,1)S(1)} %get-tuple-element.18), channel_id=1, source_target_pairs={{0,48},{1,49},{2,50},{3,51},{4,52},{5,53},{6,54},{7,55},{8,56},{9,... | collective-permute-start | bytes 393224 | tf_op jit(solution)/shard_map/ppermute | solution.py:192
  52.8 7.9 %collective-permute-start.8 = (bf16[512,128]{1,0:T(8,128)(2,1)S(1)}, bf16[512,128]{1,0:T(8,128)(2,1)S(1)}, u32[]{:S(2)}, u32[]{:S(2)}) collective-permute-start(bf16[512,128]{1,0:T(8,128)(2,1)S(1)} %get-tuple-element.17), channel_id=1, source_target_pairs={{0,32},{1,33},{2,34},{3,35},{4,36},{5,37},{6,38},{7,39},{8,40},{9,... | collective-permute-start | bytes 393224 | tf_op jit(solution)/shard_map/ppermute | solution.py:192
  53.6 8.8 %collective-permute-start.9 = (bf16[512,128]{1,0:T(8,128)(2,1)S(1)}, bf16[512,128]{1,0:T(8,128)(2,1)S(1)}, u32[]{:S(2)}, u32[]{:S(2)}) collective-permute-start(bf16[512,128]{1,0:T(8,128)(2,1)S(1)} %get-tuple-element.19), channel_id=1, source_target_pairs={{0,16},{1,17},{2,18},{3,19},{4,20},{5,21},{6,22},{7,23},{8,24},{9,... | collective-permute-start | bytes 393224 | tf_op jit(solution)/shard_map/ppermute | solution.py:192
  62.5 11.0 %copy-start.1 = (bf16[512,256]{1,0:T(8,128)(2,1)S(1)}, bf16[512,256]{1,0:T(8,128)(2,1)}, u32[]{:S(2)}) copy-start(bf16[512,256]{1,0:T(8,128)(2,1)} %refs_4_.1) | copy-start | bytes 786436
  62.5 9.6 %collective-permute-start.11 = (bf16[512,128]{1,0:T(8,128)(2,1)S(1)}, bf16[512,128]{1,0:T(8,128)(2,1)S(1)}, u32[]{:S(2)}, u32[]{:S(2)}) collective-permute-start(bf16[512,128]{1,0:T(8,128)(2,1)S(1)} %fusion.10.refs_0_), channel_id=1, source_target_pairs={{0,64},{64,128},{128,192},{192,0},{1,65},{65,129},{129,193},{193,1... | collective-permute-start | bytes 393224 | tf_op jit(solution)/shard_map/ppermute | solution.py:195
  64.3 9.1 %collective-permute-start.12 = (bf16[512,128]{1,0:T(8,128)(2,1)S(1)}, bf16[512,128]{1,0:T(8,128)(2,1)S(1)}, u32[]{:S(2)}, u32[]{:S(2)}) collective-permute-start(bf16[512,128]{1,0:T(8,128)(2,1)S(1)} %fusion.10.refs_0_), channel_id=1, source_target_pairs={{0,128},{64,192},{128,0},{192,64},{1,129},{65,193},{129,1},{193,65... | collective-permute-start | bytes 393224 | tf_op jit(solution)/shard_map/ppermute | solution.py:195
  67.2 6.2 %collective-permute-start.13 = (bf16[512,128]{1,0:T(8,128)(2,1)S(1)}, bf16[512,128]{1,0:T(8,128)(2,1)S(1)}, u32[]{:S(2)}, u32[]{:S(2)}) collective-permute-start(bf16[512,128]{1,0:T(8,128)(2,1)S(1)} %fusion.10.refs_0_), channel_id=1, source_target_pairs={{0,192},{64,0},{128,64},{192,128},{1,193},{65,1},{129,65},{193,129... | collective-permute-start | bytes 393224 | tf_op jit(solution)/shard_map/ppermute | solution.py:195

commit v2 on v0

v2 whole, which is shorter than its diff:
```python
import functools

import jax
import jax.numpy as jnp
from jax import lax
from jax.experimental import pallas as pl
from jax.experimental.pallas import tpu as pltpu
from jax.sharding import PartitionSpec as P

NX, NZ, NC = 4, 8, 2
CAP = 64
BLOCK = NZ * CAP
CHIPS = NX * NZ
MSG = NC * CAP + 8
BF, F32 = jnp.bfloat16, jnp.float32


def iota(shape, dim):
    return lax.broadcasted_iota(jnp.int32, shape, dim)


def one_hot(mask):
    return jnp.where(mask, 1.0, 0.0).astype(BF)


def pack_kernel(side, owner_ref, slot_ref, press_ref, out_ref):
    panels, cases = press_ref.shape
    me = lax.axis_index("se")
    owner = owner_ref[...]
    mine = ((owner ^ me) & 1) == side
    chip = jnp.where(mine, owner >> 1, -1)
    part = jnp.where(mine, owner >> 4, -1)
    near = (owner >> 1) & (NZ - 1)
    oh = jnp.where(iota((CHIPS, panels), 0) == chip, 1.0, 0.0)
    width = 256
    ohs = [oh[:, b * width : (b + 1) * width] for b in range(panels // width)]
    before = one_hot(iota((width, width), 0) < iota((width, width), 1))
    counts = jnp.dot(jnp.concatenate(ohs, axis=0).astype(BF), before, preferred_element_type=F32)
    start, ranks = jnp.zeros((CHIPS, 1), F32), []
    for b, piece in enumerate(ohs):
        count = counts[b * CHIPS : (b + 1) * CHIPS]
        ranks.append(jnp.sum(piece * (count + start), axis=0, keepdims=True))
        start = start + count[:, width - 1 :] + piece[:, width - 1 :]
    rank = jnp.concatenate(ranks, axis=1).astype(jnp.int32)
    place = one_hot(iota((BLOCK, panels), 0) == near * CAP + rank)

    value = (slot_ref[...] - 256).astype(F32)
    out_ref[CHIPS * CAP :, :] = lax.dot_general(
        (oh * value).astype(BF),
        one_hot(iota((128, panels), 0) == side * CAP + rank),
        (((1,), (1,)), ((), ())),
        preferred_element_type=F32,
    ).astype(BF)

    parts = jnp.transpose(jnp.broadcast_to(part.astype(F32), (128, panels)))
    press = press_ref[...]
    for j in range(0, NX, 2):
        both = [press * one_hot(parts == i) for i in (j, j + 1)]
        rows = jnp.dot(place, jnp.concatenate(both, axis=1), preferred_element_type=F32)
        for i in (j, j + 1):
            out_ref[i * BLOCK : (i + 1) * BLOCK, :] = rows[:, (i - j) * cases : (i - j + 1) * cases].astype(BF)


def pack(side, owner, slot, press):
    panels, cases = press.shape
    return pl.pallas_call(
        functools.partial(pack_kernel, side),
        out_shape=jax.ShapeDtypeStruct((CHIPS * CAP + CHIPS, cases), BF),
        compiler_params=pltpu.CompilerParams(vmem_limit_bytes=32 << 20),
        cost_estimate=pl.CostEstimate(
            flops=2 * CHIPS * CAP * panels * cases, bytes_accessed=2 << 20, transcendentals=0
        ),
        name="pack",
    )(owner, slot, press)


def scatter_kernel(msg_ref, out_ref):
    points, cases = out_ref.shape
    point = iota((points, 128), 0) - 256
    ohs, data = [], []
    for j in range(CHIPS):
        slots = msg_ref[j, NC * CAP :, :].astype(F32)[:1, :].astype(jnp.int32)
        ohs.append(one_hot(point == slots))
        data.append(msg_ref[j, : NC * CAP, :])
    out_ref[...] = jnp.dot(
        jnp.concatenate(ohs, axis=1), jnp.concatenate(data, axis=0), preferred_element_type=F32
    ).astype(BF)


def scatter(messages, points):
    cases = messages.shape[2]
    return pl.pallas_call(
        scatter_kernel,
        out_shape=jax.ShapeDtypeStruct((points, cases), BF),
        compiler_params=pltpu.CompilerParams(vmem_limit_bytes=32 << 20),
        cost_estimate=pl.CostEstimate(
            flops=2 * points * CHIPS * NC * CAP * cases, bytes_accessed=2 << 20, transcendentals=0
        ),
        name="scatter",
    )(messages)


def finish_kernel(live_ref, *refs):
    loads, (comb_ref, mat_ref, out_ref) = refs[:NX], refs[NX:]
    y = lax.axis_index("case")
    cases = loads[0].shape[1]
    total = None
    for k in range(len(loads)):
        block = pl.multiple_of(((y - k) & 3) * cases, cases)
        term = jnp.dot(loads[k][...], comb_ref[pl.ds(block, cases), :], preferred_element_type=F32)
        total = term if total is None else total + term
    rows = out_ref.shape[0]
    out = jnp.dot(mat_ref[...], total.astype(BF), preferred_element_type=F32)
    live = y * rows + iota(out.shape, 0) < live_ref[0]
    out_ref[...] = jnp.where(live, out, 0.0).astype(BF)


def finish(live, loads, comb, mat):
    vmem = pl.BlockSpec(memory_space=pltpu.VMEM)
    return pl.pallas_call(
        finish_kernel,
        in_specs=[pl.BlockSpec(memory_space=pltpu.SMEM)] + [vmem] * (len(loads) + 2),
        out_specs=vmem,
        out_shape=jax.ShapeDtypeStruct((mat.shape[0], comb.shape[1]), BF),
        compiler_params=pltpu.CompilerParams(vmem_limit_bytes=32 << 20),
        cost_estimate=pl.CostEstimate(flops=400 << 20, bytes_accessed=3 << 20, transcendentals=0),
        name="finish",
    )(live, *loads, comb, mat)


def se_index(x, z, c):
    return (x * NZ + z) * NC + c


SAME_CORE = [[se_index(x, z, c) for x in range(NX) for z in range(NZ)] for c in range(NC)]
OTHER_CORE = [(i, i ^ 1) for i in range(NX * NZ * NC)]


def per_device(
    panel_press, panel_owner, panel_slot, elem_count, flexibility, stress_matrix, combination
):
    panels, cases = panel_press.shape
    points = flexibility.shape[2]
    owner, slot = panel_owner.reshape(1, panels), panel_slot.reshape(1, panels)
    theirs = lax.ppermute(pack(1, owner, slot, panel_press), "se", OTHER_CORE)
    ours = pack(0, owner, slot, panel_press)
    slots = ours[CHIPS * CAP :] + theirs[CHIPS * CAP :]
    messages = jnp.concatenate(
        [
            ours[: CHIPS * CAP].reshape(CHIPS, CAP, cases),
            theirs[: CHIPS * CAP].reshape(CHIPS, CAP, cases),
            jnp.broadcast_to(slots[:, None, :], (CHIPS, MSG - NC * CAP, cases)),
        ],
        axis=1,
    )
    messages = lax.all_to_all(messages, "se", 0, 0, axis_index_groups=SAME_CORE, tiled=True)
    loads = [scatter(messages, points)]
    for k in (1, 2, 3):
        loads.append(lax.ppermute(loads[0], "case", [(y, (y + k) % 4) for y in range(4)]))
    mat = jnp.dot(
        stress_matrix[0], flexibility[0], preferred_element_type=F32
    ).astype(BF)
    return finish(elem_count, loads, combination, mat)[None]


def solution(mesh):
    return jax.shard_map(
        per_device,
        mesh=mesh,
        in_specs=(
            P("se", "case"),
            P("se", None),
            P("se"),
            P("se"),
            P("se", None, None),
            P("se", "case", None),
            P(),
        ),
        out_specs=P("se", "case", None),
        check_vma=False,
    )
```

time: 273 us -> 63.7 us (0.23)
  waiting for transfers between devices: 228 us -> 0.98 us
  blocking collectives: 0 us -> 42.6 us
  other arithmetic: 20.2 us -> 0.09 us
  between operations: 14.1 us -> 0.77 us
  matrix products: 10.1 us -> 2.85 us
  Pallas kernels: 0 us -> 7.16 us
  starting transfers between devices: 0.04 us -> 6 us
    reduce_scatter x1 -> x0, waiting for transfers between devices: 191 us -> none  [per_device(): loads = lax.psum_scatter(load_sums, 'se', scatter_dimension=0, tiled=True)]
    all_to_all x0 -> x1, blocking collectives: none -> 42.6 us  [per_device(): lax.all_to_all(messages, 'se', 0, 0, axis_index_groups=SAME_CORE, tiled=T...]
    all_gather x1 -> x0, waiting for transfers between devices: 36.4 us -> none  [per_device(): lax.all_gather(displacement, 'case', axis=1, tiled=True)]
    scatter-add x1 -> x0, other arithmetic: 18.6 us -> none  [per_device(): jax.ops.segment_sum(panel_press.astype(jnp.float32), segment_ids, num_seg...]
    dot_general x2 -> x1, matrix products: 10.1 us -> 2.85 us  [per_device(): jnp.dot(stress_matrix[0], flexibility[0], preferred_element_type=F32)]
    pallas_call x0 -> x4, Pallas kernels: none -> 7.16 us  [the longest x2 3.86 us: pack(): pl.pallas_call(functools.partial(pack_kernel, side), out_shape=jax.ShapeD...]
    ppermute x0 -> x4, starting transfers between devices: none -> 6 us  [the longest x3 5.9 us: per_device(): lax.ppermute(loads[0], 'case', [(y, (y + k) % 4) for y in range(4)])]
  transfers between devices with their start and end apart: 2 -> 4, of which waited for: 2 -> 1; matrix products, arithmetic and copies ran while one was open for 0% -> 5% of each run, Pallas kernels for 0% -> 3%
where the time goes in v2:
time: 63.7 us; the launch traced here: 63.2 us
  blocking collectives  42.6 us (67%)
  Pallas kernels  7.16 us (11%)
  starting transfers between devices  6 us (9%)
  matrix products  2.85 us (4%)
  local copies, waits for them, and re-layouts  2.69 us (4%)
  waiting for transfers between devices  0.98 us (2%)
  between operations  0.77 us (1%)
    all_to_all x1, blocking collectives, per_device(): lax.all_to_all(messages, 'se', 0, 0, axis_index_groups=SAME_CORE, tiled=T...  42.6 us
    ppermute x3, starting transfers between devices, per_device(): lax.ppermute(loads[0], 'case', [(y, (y + k) % 4) for y in range(4)])  5.9 us
    pallas_call x2, Pallas kernels, pack(): pl.pallas_call(functools.partial(pack_kernel, side), out_shape=jax.ShapeD...  3.86 us
    dot_general x1, matrix products, per_device(): jnp.dot(stress_matrix[0], flexibility[0], preferred_element_type=F32)  2.85 us
    unnamed x14, local copies, waits for them, and re-layouts  2.61 us
    pallas_call x1, Pallas kernels, finish(): pl.pallas_call(finish_kernel, in_specs=[pl.BlockSpec(memory_space=pltpu.S...  2.06 us
  transfers between devices with their start and end apart: 4, of which 1 were waited for; matrix products, arithmetic and copies ran while one was open for 5% of the time, Pallas kernels for 3%

profile of v2, /device:TPU:32, one launch (start us, length us, event | category | flops | bytes accessed | tf_op | source)
XLA Modules:
  0.0 63.2 jit_solution(5513697647657001572)
XLA Ops:
  0.0 0.0 copy-start
  0.0 1.2 %copy-done.2 = bf16[2048,128]{1,0:T(8,128)(2,1)S(1)} copy-done((bf16[2048,128]{1,0:T(8,128)(2,1)S(1)}, bf16[2048,128]{1,0:T(8,128)(2,1)}, u32[]{:S(2)}) %copy-start.2) | copy-done | bytes 524312
  1.2 0.7 %copy-done.3 = s32[2048,1]{0,1:T(1,128)S(1)} copy-done((s32[2048,1]{0,1:T(1,128)S(1)}, s32[2048,1]{0,1:T(1,128)}, u32[]{:S(2)}) %copy-start.3) | copy-done | bytes 8216
  1.9 0.7 %copy-done.4 = s32[2048]{0:T(1024)S(1)} copy-done((s32[2048]{0:T(1024)S(1)}, s32[2048]{0:T(1024)}, u32[]{:S(2)}) %copy-start.4) | copy-done | bytes 8216
  2.6 1.9 %pack.3 = bf16[2080,128]{1,0:T(8,128)(2,1)S(1)} custom-call(s32[1,2048]{1,0:T(1,128)S(1)} %bitcast.15, s32[1,2048]{1,0:T(1,128)S(1)} %bitcast.17, bf16[2048,128]{1,0:T(8,128)(2,1)S(1)} %copy-done.2), custom_call_target="tpu_custom_call" | custom-call | flops 1073741824 | bytes 2097152 | tf_op jit(solution)/shard_map/pack/pallas_call | solution.py:66
  4.5 0.1 collective-permute-start
  4.6 1.9 %pack.2 = bf16[2080,128]{1,0:T(8,128)(2,1)S(1)} custom-call(s32[1,2048]{1,0:T(1,128)S(1)} %bitcast.16, s32[1,2048]{1,0:T(1,128)S(1)} %bitcast.18, bf16[2048,128]{1,0:T(8,128)(2,1)S(1)} %copy-done.2), custom_call_target="tpu_custom_call" | custom-call | flops 1073741824 | bytes 2097152 | tf_op jit(solution)/shard_map/pack/pallas_call | solution.py:66
  6.6 0.0 slice-start.1
  6.6 0.0 collective-permute-done
  6.7 0.1 pad_maximum_fusion
  6.8 42.6 %all_to_all.5.msg_ref = bf16[32,136,128]{2,1,0:T(8,128)(2,1)S(1)} all-to-all(bf16[32,136,128]{2,1,0:T(8,128)(2,1)S(1)} %pad_maximum_fusion), channel_id=1, replica_groups={{0,2,4,6,8,10,12,14,16,18,20,22,24,26,28,30,32,34,36,38,40,42,44,46,48,..., dimensions={0} | all-to-all | bytes 2228224 | tf_op jit(solution)/shard_map/all_to_all | solution.py:156
  49.4 1.2 %scatter.1.refs_0_ = bf16[512,128]{1,0:T(8,128)(2,1)S(1)} custom-call(bf16[32,136,128]{2,1,0:T(8,128)(2,1)S(1)} %all_to_all.5.msg_ref), custom_call_target="tpu_custom_call" | custom-call | flops 536870912 | bytes 2097152 | tf_op jit(solution)/shard_map/scatter/pallas_call | solution.py:92
  50.7 0.0 copy-start.1
  50.7 1.7 %collective-permute-start.1 = (bf16[512,128]{1,0:T(8,128)(2,1)S(1)}, bf16[512,128]{1,0:T(8,128)(2,1)S(1)}, u32[]{:S(2)}, u32[]{:S(2)}) collective-permute-start(bf16[512,128]{1,0:T(8,128)(2,1)S(1)} %scatter.1.refs_0_), channel_id=1, source_target_pairs={{0,64},{64,128},{128,192},{192,0},{1,65},{65,129},{129,193},{193,1... | collective-permute-start | bytes 393224 | tf_op jit(solution)/shard_map/ppermute | solution.py:159
  52.3 2.9 %collective-permute-start.2 = (bf16[512,128]{1,0:T(8,128)(2,1)S(1)}, bf16[512,128]{1,0:T(8,128)(2,1)S(1)}, u32[]{:S(2)}, u32[]{:S(2)}) collective-permute-start(bf16[512,128]{1,0:T(8,128)(2,1)S(1)} %scatter.1.refs_0_), channel_id=1, source_target_pairs={{0,128},{64,192},{128,0},{192,64},{1,129},{65,193},{129,1},{193,65... | collective-permute-start | bytes 393224 | tf_op jit(solution)/shard_map/ppermute | solution.py:159
  55.2 1.3 %collective-permute-start.3 = (bf16[512,128]{1,0:T(8,128)(2,1)S(1)}, bf16[512,128]{1,0:T(8,128)(2,1)S(1)}, u32[]{:S(2)}, u32[]{:S(2)}) collective-permute-start(bf16[512,128]{1,0:T(8,128)(2,1)S(1)} %scatter.1.refs_0_), channel_id=1, source_target_pairs={{0,192},{64,0},{128,64},{192,128},{1,193},{65,1},{129,65},{193,129... | collective-permute-start | bytes 393224 | tf_op jit(solution)/shard_map/ppermute | solution.py:159
  56.6 0.0 copy-done
  56.6 0.0 slice-done
  56.6 0.0 slice-done.1
  56.6 2.9 %fusion.3.refs_5_ = bf16[1024,512]{1,0:T(8,128)(2,1)S(1)} fusion(bf16[1,2560,512]{2,1,0:T(8,128)(2,1)S(1)} %copy-done, bf16[1,1024,2560]{2,1,0:T(8,128)(2,1)S(1)} %bitcast.22), kind=kOutput, calls=%fused_computation.3 | convolution fusion | flops 2684878848 | bytes 8912896 | tf_op jit(solution)/shard_map/dot_general | solution.py:160
  60.1 0.0 collective-permute-done.1.refs_1_
  60.1 1.0 %collective-permute-done.2.refs_2_ = bf16[512,128]{1,0:T(8,128)(2,1)S(1)} collective-permute-done((bf16[512,128]{1,0:T(8,128)(2,1)S(1)}, bf16[512,128]{1,0:T(8,128)(2,1)S(1)}, u32[]{:S(2)}, u32[]{:S(2)}) %collective-permute-start.2) | collective-permute-done | bytes 131104 | tf_op jit(solution)/shard_map/ppermute | solution.py:159
  61.1 0.0 collective-permute-done.3.refs_3_
  61.1 2.1 %finish.1 = bf16[1024,256]{1,0:T(8,128)(2,1)} custom-call(s32[1]{0:T(128)S(6)} %copy.8.live_ref, bf16[512,128]{1,0:T(8,128)(2,1)S(1)} %scatter.1.refs_0_, bf16[512,128]{1,0:T(8,128)(2,1)S(1)} %collective-permute-done.1.refs_1_, bf16[512,128]{1,0:T(8,128)(2,1)S(1)} %collective-permute-done.2.refs_2_, bf16[512,128]{1,0:T(8,128)(2,1)S(1)} %collective-permute-done.3.refs_3_, ...), custom_call_target="tpu_custom_call" | custom-call | flops 419430400 | bytes 3145728 | tf_op jit(solution)/shard_map/finish/pallas_call | solution.py:120
  (10 shorter events, 0.1 us)
Async XLA Ops:
  0.0 56.6 %copy-start = (bf16[1,2560,512]{2,1,0:T(8,128)(2,1)S(1)}, bf16[1,2560,512]{2,1,0:T(8,128)(2,1)}, u32[]{:S(2)}) copy-start(bf16[1,2560,512]{2,1,0:T(8,128)(2,1)} %param.11) | copy-start | bytes 7864324
  0.0 1.2 %copy-start.2 = (bf16[2048,128]{1,0:T(8,128)(2,1)S(1)}, bf16[2048,128]{1,0:T(8,128)(2,1)}, u32[]{:S(2)}) copy-start(bf16[2048,128]{1,0:T(8,128)(2,1)} %press_ref.3) | copy-start | bytes 1572868
  1.2 0.7 %copy-start.3 = (s32[2048,1]{0,1:T(1,128)S(1)}, s32[2048,1]{0,1:T(1,128)}, u32[]{:S(2)}) copy-start(s32[2048,1]{0,1:T(1,128)} %param.8) | copy-start | bytes 24580
  1.9 0.7 %copy-start.4 = (s32[2048]{0:T(1024)S(1)}, s32[2048]{0:T(1024)}, u32[]{:S(2)}) copy-start(s32[2048]{0:T(1024)} %param.9) | copy-start | bytes 24580
  2.6 54.0 %slice-start = ((s8[5242880]{0:T(1024)(128)(4,1)}), s8[4194304]{0:T(1024)(128)(4,1)S(1)}, s32[]{:S(2)}) async-start(s8[5242880]{0:T(1024)(128)(4,1)} %bitcast.21), calls=%async_computation.1 | async-start | bytes 8388608
  4.5 2.1 %collective-permute-start = (bf16[2080,128]{1,0:T(8,128)(2,1)S(1)}, bf16[2080,128]{1,0:T(8,128)(2,1)S(1)}, u32[]{:S(2)}, u32[]{:S(2)}) collective-permute-start(bf16[2080,128]{1,0:T(8,128)(2,1)S(1)} %pack.3), channel_id=1, source_target_pairs={{0,1},{1,0},{2,3},{3,2},{4,5},{5,4},{6,7},{7,6},{8,9},{9,8},{10,11... | collective-permute-start | bytes 1597448 | tf_op jit(solution)/shard_map/ppermute | solution.py:145
  6.6 50.0 %slice-start.1 = ((s8[5242880]{0:T(1024)(128)(4,1)}), s8[1048576]{0:T(1024)(128)(4,1)S(1)}, s32[]{:S(2)}) async-start(s8[5242880]{0:T(1024)(128)(4,1)} %bitcast.21), calls=%async_computation.2 | async-start | bytes 2097152
  50.7 10.4 %copy-start.1 = (bf16[512,256]{1,0:T(8,128)(2,1)S(1)}, bf16[512,256]{1,0:T(8,128)(2,1)}, u32[]{:S(2)}) copy-start(bf16[512,256]{1,0:T(8,128)(2,1)} %refs_4_.1) | copy-start | bytes 786436
  50.7 9.4 %collective-permute-start.1 = (bf16[512,128]{1,0:T(8,128)(2,1)S(1)}, bf16[512,128]{1,0:T(8,128)(2,1)S(1)}, u32[]{:S(2)}, u32[]{:S(2)}) collective-permute-start(bf16[512,128]{1,0:T(8,128)(2,1)S(1)} %scatter.1.refs_0_), channel_id=1, source_target_pairs={{0,64},{64,128},{128,192},{192,0},{1,65},{65,129},{129,193},{193,1... | collective-permute-start | bytes 393224 | tf_op jit(solution)/shard_map/ppermute | solution.py:159
  52.3 8.8 %collective-permute-start.2 = (bf16[512,128]{1,0:T(8,128)(2,1)S(1)}, bf16[512,128]{1,0:T(8,128)(2,1)S(1)}, u32[]{:S(2)}, u32[]{:S(2)}) collective-permute-start(bf16[512,128]{1,0:T(8,128)(2,1)S(1)} %scatter.1.refs_0_), channel_id=1, source_target_pairs={{0,128},{64,192},{128,0},{192,64},{1,129},{65,193},{129,1},{193,65... | collective-permute-start | bytes 393224 | tf_op jit(solution)/shard_map/ppermute | solution.py:159
  55.2 5.9 %collective-permute-start.3 = (bf16[512,128]{1,0:T(8,128)(2,1)S(1)}, bf16[512,128]{1,0:T(8,128)(2,1)S(1)}, u32[]{:S(2)}, u32[]{:S(2)}) collective-permute-start(bf16[512,128]{1,0:T(8,128)(2,1)S(1)} %scatter.1.refs_0_), channel_id=1, source_target_pairs={{0,192},{64,0},{128,64},{192,128},{1,193},{65,1},{129,65},{193,129... | collective-permute-start | bytes 393224 | tf_op jit(solution)/shard_map/ppermute | solution.py:159

commit v3 on v0

v3 whole, which is shorter than its diff:
```python
import jax
import jax.numpy as jnp
from jax import lax
from jax.experimental import pallas as pl
from jax.experimental.pallas import tpu as pltpu
from jax.sharding import PartitionSpec as P

NX, NZ, NC, NY = 4, 8, 2, 4
CAP = 64
CHIPS = NX * NZ
LANES, HALF = 128, 64
PER = CAP // 2
GROUP = 16
MSG = NC * PER + 8
OUT_PARTS = 4
FETCH_VMEM = 52
BF, F32 = jnp.bfloat16, jnp.float32


def iota(shape, dim):
    return lax.broadcasted_iota(jnp.int32, shape, dim)


def one_hot(mask):
    return jnp.where(mask, 1.0, 0.0).astype(BF)


def dot(a, b):
    return jnp.dot(a, b, preferred_element_type=F32)


def call(kernel, out_shape, args, flops, name, in_specs=None, vmem=32, **more):
    if in_specs is not None:
        more["in_specs"] = in_specs
    return pl.pallas_call(
        kernel,
        out_shape=out_shape,
        compiler_params=pltpu.CompilerParams(vmem_limit_bytes=vmem << 20),
        cost_estimate=pl.CostEstimate(flops=flops, bytes_accessed=2 << 20, transcendentals=0),
        name=name,
        **more,
    )(*args)


def project_kernel(press_hbm, comb_hbm, own_ref, *refs):
    send_refs, (press_ref, comb_ref, sems) = refs[: NY - 1], refs[NY - 1 :]
    panels, cases = press_ref.shape
    combos = comb_ref.shape[1]
    y = lax.axis_index("case")
    at = pl.ds(pl.multiple_of(y * cases, cases), cases)
    comb_copy = pltpu.make_async_copy(comb_hbm.at[at], comb_ref, sems.at[0])
    press_copy = pltpu.make_async_copy(press_hbm, press_ref, sems.at[1])
    comb_copy.start()
    press_copy.start()
    source, target = iota((combos, NY * LANES), 0), iota((combos, NY * LANES), 1)
    lane = target & (LANES - 1)
    turn = 1 - 2 * (lax.axis_index("se") & 1)
    column = ((target >> 7) * (turn * HALF) + (lane & (HALF - 1)) + y * HALF) & (combos - 1)
    left = one_hot((source == column) & (lane < HALF))
    right = one_hot((source == column) & (lane >= HALF))
    comb_copy.wait()
    mine = comb_ref[...]
    first, second = dot(mine, left).astype(BF), dot(mine, right).astype(BF)
    press_copy.wait()
    half = panels // 2
    both = jnp.concatenate([press_ref[:half, :], press_ref[half:, :]], axis=1)
    product = dot(both, jnp.concatenate([first, second], axis=0))
    own_ref[...] = product[:, :LANES]
    for k, ref in enumerate(send_refs):
        ref[...] = product[:, (k + 1) * LANES : (k + 2) * LANES].astype(BF)


def rank_kernel(owner_ref, slot_ref, place_ref, masks_ref, meta_ref):
    panels = owner_ref.shape[1]
    me = lax.axis_index("se")
    owner = owner_ref[...]
    side = (owner ^ me) & 1
    chip = owner >> 1
    owners = CHIPS * NC
    oh = jnp.where(iota((owners, panels), 0) == side * CHIPS + chip, 1.0, 0.0)
    width = 256
    ohs = [oh[:, b * width : (b + 1) * width] for b in range(panels // width)]
    before = one_hot(iota((width, width), 0) < iota((width, width), 1))
    counts = dot(jnp.concatenate(ohs, axis=0).astype(BF), before)
    start, ranks = jnp.zeros((owners, 1), F32), []
    for b, piece in enumerate(ohs):
        count = counts[b * owners : (b + 1) * owners]
        ranks.append(jnp.sum(piece * (count + start), axis=0, keepdims=True))
        start = start + count[:, width - 1 :] + piece[:, width - 1 :]
    rank = jnp.concatenate(ranks, axis=1).astype(jnp.int32)
    low, high = rank & (PER - 1), rank // PER
    place_ref[...] = one_hot(iota((GROUP * PER, panels), 0) == (chip & (GROUP - 1)) * PER + low)
    lanes = high * HALF + side * PER + low
    meta_ref[...] = lax.dot_general(
        (oh * (slot_ref[...] - 256).astype(F32)).astype(BF),
        one_hot(iota((LANES, panels), 0) == lanes),
        (((1,), (1,)), ((), ())),
        preferred_element_type=F32,
    ).astype(BF)
    group = side * 4 + (chip // GROUP) * 2 + high
    groups = jnp.transpose(jnp.broadcast_to(group.astype(F32), (LANES, panels)))
    part = (iota((1, LANES), 1) // HALF).astype(F32)
    for s in range(NC):
        for h in range(2):
            masks_ref[s, :, h * LANES : (h + 1) * LANES] = one_hot(groups == part + (s * 4 + h * 2))


def place_rows(rows, place_ref, mask_ref, meta_ref, out_ref):
    lane = iota(rows.shape, 1)
    turned = pltpu.roll(rows, HALF, 1)
    first = jnp.where(lane < HALF, rows, turned).astype(BF)
    second = jnp.where(lane < HALF, turned, rows).astype(BF)
    each = jnp.concatenate([first, second], axis=0)
    placed = dot(place_ref[...], jnp.concatenate([each, each], axis=1) * mask_ref[0])
    size = GROUP * PER
    for h in range(2):
        out_ref[h * size : (h + 1) * size, :] = placed[:, h * LANES : (h + 1) * LANES].astype(BF)
    out_ref[2 * size :, :] = meta_ref[...]


def sum_and_pack(own_ref, r1_ref, r2_ref, r3_ref, place_ref, mask_ref, meta_ref, out_ref, rows_ref):
    rows = own_ref[...] + r1_ref[...].astype(F32) + r2_ref[...].astype(F32) + r3_ref[...].astype(F32)
    rows_ref[...] = rows
    place_rows(rows, place_ref, mask_ref, meta_ref, out_ref)


def pack_kernel(rows_ref, place_ref, mask_ref, meta_ref, out_ref):
    place_rows(rows_ref[...], place_ref, mask_ref, meta_ref, out_ref)


def pack(kernel, side, rows, place, masks, meta, out_shape):
    whole = [pl.BlockSpec(a.shape, lambda i: (0, 0)) for a in rows]
    return call(
        kernel,
        out_shape,
        (*rows, place, masks, meta),
        1 << 30,
        "pack",
        grid=(1,),
        in_specs=whole
        + [
            pl.BlockSpec(place.shape, lambda i: (0, 0)),
            pl.BlockSpec((1,) + masks.shape[1:], lambda i: (side, 0, 0)),
            pl.BlockSpec((CHIPS, LANES), lambda i: (side, 0)),
        ],
        out_specs=jax.tree.map(lambda s: pl.BlockSpec(s.shape, lambda i: (0, 0)), out_shape),
    )


def scatter_kernel(msg_ref, out_ref):
    points = 2 * out_ref.shape[0]
    point = (iota((points, LANES), 0) - 256).astype(F32).astype(BF)
    left = iota((1, LANES), 1) < HALF
    one, zero = jnp.ones((), BF), jnp.zeros((), BF)
    lows, highs, data = [], [], []
    for j in range(0, CHIPS, 2):
        a, b = (
            msg_ref[i, NC * PER :, :].astype(F32)[:1, :] for i in (j, j + 1)
        )
        low = jnp.where(left, a, pltpu.roll(b, HALF, 1)).astype(BF)
        high = jnp.where(left, pltpu.roll(a, HALF, 1), b).astype(BF)
        lows.append(jnp.where(point == low, one, zero))
        highs.append(jnp.where(point == high, one, zero))
        data += [msg_ref[i, : NC * PER, :] for i in (j, j + 1)]
    rows = jnp.concatenate(data, axis=0)
    total = dot(jnp.concatenate(lows, axis=1), rows)
    total = total + pltpu.roll(dot(jnp.concatenate(highs, axis=1), rows), HALF, 1)
    half = points // 2
    right = pltpu.roll(total[half:], HALF, 1)
    out_ref[...] = jnp.where(left, total[:half], right).astype(BF)


def finish_kernel(live_ref, *refs):
    loads, (mat_ref, out_ref, block_ref, sems) = refs[:NY], refs[NY:]
    y = lax.axis_index("case")
    rows, combos = block_ref.shape
    source, target = iota((NY * LANES, combos), 0), iota((NY * LANES, combos), 1)
    lane = source & (LANES - 1)
    turn = 1 - 2 * (lax.axis_index("se") & 1)
    hit = ((y - turn * (source >> 7)) & (NY - 1)) * HALF + (lane & (HALF - 1)) == target
    every = jnp.concatenate([ref[...] for ref in loads], axis=1)
    upper = dot(every, one_hot(hit & (lane < HALF)))
    lower = dot(every, one_hot(hit & (lane >= HALF)))
    total = jnp.concatenate([upper, lower], axis=0).astype(BF)
    part = rows // OUT_PARTS
    copies = []
    for p in range(OUT_PARTS):
        at = pl.ds(p * part, part)
        out = dot(mat_ref[at, :], total)
        live = y * rows + p * part + iota(out.shape, 0) < live_ref[0]
        block_ref[at, :] = jnp.where(live, out, 0.0).astype(BF)
        copies.append(pltpu.make_async_copy(block_ref.at[at], out_ref.at[at], sems.at[p]))
        copies[-1].start()
    for copy in copies:
        copy.wait()


def se_index(x, z, c):
    return (x * NZ + z) * NC + c


SAME_CORE = [[se_index(x, z, c) for x in range(NX) for z in range(NZ)] for c in range(NC)]
OTHER_CORE = [(i, i ^ 1) for i in range(NX * NZ * NC)]


def along_y(a, k):
    owners = NX * NZ * NC
    pairs = [
        (y * owners + i, (y + (k if i % NC == 0 else -k)) % NY * owners + i)
        for y in range(NY)
        for i in range(owners)
    ]
    return lax.ppermute(a, ("case", "se"), pairs)


def shape(*dims, dtype=BF):
    return jax.ShapeDtypeStruct(dims, dtype)


def per_device(
    panel_press, panel_owner, panel_slot, elem_count, flexibility, stress_matrix, combination
):
    panels = panel_press.shape[0]
    points, combos = flexibility.shape[2], combination.shape[1]
    half = panels // 2
    own, *sent = call(
        project_kernel,
        [shape(half, LANES, dtype=F32)] + [shape(half, LANES)] * (NY - 1),
        (panel_press, combination),
        1 << 28,
        "project",
        in_specs=[pl.BlockSpec(memory_space=pltpu.HBM)] * 2,
        vmem=FETCH_VMEM,
        scratch_shapes=[
            pltpu.VMEM(panel_press.shape, BF),
            pltpu.VMEM((panel_press.shape[1], combos), BF),
            pltpu.SemaphoreType.DMA((2,)),
        ],
    )
    parts = [own] + [along_y(sent[k - 1], k) for k in range(1, NY)]
    place, masks, meta = call(
        rank_kernel,
        (shape(GROUP * PER, panels), shape(NC, panels, 2 * LANES), shape(NC * CHIPS, LANES)),
        (panel_owner.reshape(1, panels), panel_slot.reshape(1, panels)),
        1 << 28,
        "rank",
    )
    mat = dot(stress_matrix[0], flexibility[0]).astype(BF)
    parts, mat = lax.optimization_barrier((parts, mat))
    packed = shape(CHIPS * PER + CHIPS, LANES)
    theirs, rows = pack(
        sum_and_pack, 1, parts, place, masks, meta, (packed, shape(half, LANES, dtype=F32))
    )
    theirs = lax.ppermute(theirs, "se", OTHER_CORE)
    ours = pack(pack_kernel, 0, [rows], place, masks, meta, packed)
    slots = ours[CHIPS * PER :] + theirs[CHIPS * PER :]
    messages = jnp.concatenate(
        [
            ours[: CHIPS * PER].reshape(CHIPS, PER, LANES),
            theirs[: CHIPS * PER].reshape(CHIPS, PER, LANES),
            jnp.broadcast_to(slots[:, None, :], (CHIPS, MSG - NC * PER, LANES)),
        ],
        axis=1,
    )
    messages = lax.all_to_all(messages, "se", 0, 0, axis_index_groups=SAME_CORE, tiled=True)
    loads = [call(scatter_kernel, shape(points // 2, LANES), (messages,), 1 << 30, "scatter")]
    loads += [along_y(loads[0], k) for k in range(1, NY)]
    local = mat.shape[0]
    vmem = pl.BlockSpec(memory_space=pltpu.VMEM)
    out = call(
        finish_kernel,
        shape(local, combos),
        (elem_count, *loads, mat),
        1 << 28,
        "finish",
        in_specs=[pl.BlockSpec(memory_space=pltpu.SMEM)] + [vmem] * (NY + 1),
        out_specs=pl.BlockSpec(memory_space=pltpu.HBM),
        scratch_shapes=[pltpu.VMEM((local, combos), BF), pltpu.SemaphoreType.DMA((OUT_PARTS,))],
    )
    return out[None]


def solution(mesh):
    return jax.shard_map(
        per_device,
        mesh=mesh,
        in_specs=(
            P("se", "case"),
            P("se", None),
            P("se"),
            P("se"),
            P("se", None, None),
            P("se", "case", None),
            P(),
        ),
        out_specs=P("se", "case", None),
        check_vma=False,
    )
```

time: 273 us -> 62.4 us (0.23)
  waiting for transfers between devices: 228 us -> 6.96 us
  blocking collectives: 0 us -> 30.2 us
  other arithmetic: 20.2 us -> 0.05 us
  between operations: 14.1 us -> 0.77 us
  starting transfers between devices: 0.04 us -> 9.73 us
  Pallas kernels: 0 us -> 7.95 us
  matrix products: 10.1 us -> 5.34 us
    reduce_scatter x1 -> x0, waiting for transfers between devices: 191 us -> none  [per_device(): loads = lax.psum_scatter(load_sums, 'se', scatter_dimension=0, tiled=True)]
    all_gather x1 -> x0, waiting for transfers between devices: 36.4 us -> none  [per_device(): lax.all_gather(displacement, 'case', axis=1, tiled=True)]
    all_to_all x0 -> x1, blocking collectives: none -> 30.2 us  [per_device(): lax.all_to_all(messages, 'se', 0, 0, axis_index_groups=SAME_CORE, tiled=T...]
    scatter-add x1 -> x0, other arithmetic: 18.6 us -> none  [per_device(): jax.ops.segment_sum(panel_press.astype(jnp.float32), segment_ids, num_seg...]
    ppermute x0 -> x7, starting transfers between devices: none -> 9.73 us  [the longest x6 9.64 us: along_y(): return lax.ppermute(a, ('case', 'se'), pairs)]
    pallas_call x0 -> x6, Pallas kernels: none -> 7.95 us  [call(): pl.pallas_call(kernel, out_shape=out_shape, compiler_params=pltpu.Compile...]
    ppermute x0 -> x7, waiting for transfers between devices: none -> 6.96 us  [the longest x6 6.24 us: along_y(): return lax.ppermute(a, ('case', 'se'), pairs)]
    dot_general x2 -> x1, matrix products: 10.1 us -> 5.34 us  [dot(): return jnp.dot(a, b, preferred_element_type=F32)]
  transfers between devices with their start and end apart: 2 -> 7, of which waited for: 2 -> 5; matrix products, arithmetic and copies ran while one was open for 0% -> 9% of each run, Pallas kernels for 0% -> 4%
where the time goes in v3:
time: 62.4 us; the launch traced here: 62.2 us
  blocking collectives  30.2 us (48%)
  starting transfers between devices  9.73 us (16%)
  Pallas kernels  7.95 us (13%)
  waiting for transfers between devices  6.96 us (11%)
  matrix products  5.34 us (9%)
  local copies, waits for them, and re-layouts  1.16 us (2%)
  between operations  0.77 us (1%)
    all_to_all x1, blocking collectives, per_device(): lax.all_to_all(messages, 'se', 0, 0, axis_index_groups=SAME_CORE, tiled=T...  30.2 us
    ppermute x6, starting transfers between devices, along_y(): return lax.ppermute(a, ('case', 'se'), pairs)  9.64 us
    pallas_call x6, Pallas kernels, call(): pl.pallas_call(kernel, out_shape=out_shape, compiler_params=pltpu.Compile...  7.95 us
    ppermute x6, waiting for transfers between devices, along_y(): return lax.ppermute(a, ('case', 'se'), pairs)  6.24 us
    dot_general x1, matrix products, dot(): return jnp.dot(a, b, preferred_element_type=F32)  5.34 us
  transfers between devices with their start and end apart: 7, of which 5 were waited for; matrix products, arithmetic and copies ran while one was open for 9% of the time, Pallas kernels for 4%

profile of v3, /device:TPU:32, one launch (start us, length us, event | category | flops | bytes accessed | tf_op | source)
XLA Modules:
  0.0 62.2 jit_solution(12375534349639638602)
XLA Ops:
  0.0 0.0 copy-start
  0.0 1.1 %copy-done.1 = bf16[512,256]{1,0:T(8,128)(2,1)S(1)} copy-done((bf16[512,256]{1,0:T(8,128)(2,1)S(1)}, bf16[512,256]{1,0:T(8,128)(2,1)}, u32[]{:S(2)}) %copy-start.1) | copy-done | bytes 262168
  1.1 1.5 %project.1 = (f32[1024,128]{1,0:T(8,128)S(1)}, bf16[1024,128]{1,0:T(8,128)(2,1)S(1)}, bf16[1024,128]{1,0:T(8,128)(2,1)S(1)}, bf16[1024,128]{1,0:T(8,128)(2,1)S(1)}) custom-call(bf16[2048,128]{1,0:T(8,128)(2,1)} %press_hbm.1, bf16[512,256]{1,0:T(8,128)(2,1)S(1)} %copy-done.1), custom_call_target="tpu_custom_call" | custom-call | flops 268435456 | bytes 2097152 | tf_op jit(solution)/shard_map/project/pallas_call | solution.py:35
  2.6 1.7 %collective-permute-start = (bf16[1024,128]{1,0:T(8,128)(2,1)S(1)}, bf16[1024,128]{1,0:T(8,128)(2,1)S(1)}, u32[]{:S(2)}, u32[]{:S(2)}) collective-permute-start(bf16[1024,128]{1,0:T(8,128)(2,1)S(1)} %get-tuple-element.20), channel_id=1, source_target_pairs={{0,64},{1,193},{2,66},{3,195},{4,68},{5,197},{6,70},{7,199},{8,72}... | collective-permute-start | bytes 786440 | tf_op jit(solution)/shard_map/ppermute | solution.py:213
  4.3 2.9 %collective-permute-start.1 = (bf16[1024,128]{1,0:T(8,128)(2,1)S(1)}, bf16[1024,128]{1,0:T(8,128)(2,1)S(1)}, u32[]{:S(2)}, u32[]{:S(2)}) collective-permute-start(bf16[1024,128]{1,0:T(8,128)(2,1)S(1)} %get-tuple-element.21), channel_id=1, source_target_pairs={{0,128},{1,129},{2,130},{3,131},{4,132},{5,133},{6,134},{7,135},{8... | collective-permute-start | bytes 786440 | tf_op jit(solution)/shard_map/ppermute | solution.py:213
  7.2 1.3 %collective-permute-start.2 = (bf16[1024,128]{1,0:T(8,128)(2,1)S(1)}, bf16[1024,128]{1,0:T(8,128)(2,1)S(1)}, u32[]{:S(2)}, u32[]{:S(2)}) collective-permute-start(bf16[1024,128]{1,0:T(8,128)(2,1)S(1)} %get-tuple-element.22), channel_id=1, source_target_pairs={{0,192},{1,65},{2,194},{3,67},{4,196},{5,69},{6,198},{7,71},{8,200... | collective-permute-start | bytes 786440 | tf_op jit(solution)/shard_map/ppermute | solution.py:213
  8.6 5.3 %fusion.3.refs_4_ = bf16[1024,512]{1,0:T(8,128)(2,1)S(1)} fusion(bf16[1,2560,512]{2,1,0:T(8,128)(2,1)S(1)} %copy-done, bf16[1,1024,2560]{2,1,0:T(8,128)(2,1)} %param.12), kind=kOutput, calls=%fused_computation.3 | convolution fusion | flops 2684878848 | bytes 8912896 | tf_op jit(solution)/shard_map/dot_general | solution.py:29
  13.9 1.9 %rank.1 = (bf16[512,2048]{1,0:T(8,128)(2,1)S(1)}, bf16[2,2048,256]{2,1,0:T(8,128)(2,1)S(1)}, bf16[64,128]{1,0:T(8,128)(2,1)S(1)}) custom-call(s32[1,2048]{1,0:T(1,128)S(1)} %bitcast.15, s32[1,2048]{1,0:T(1,128)S(1)} %bitcast.16), custom_call_target="tpu_custom_call" | custom-call | flops 268435456 | bytes 2097152 | tf_op jit(solution)/shard_map/rank/pallas_call | solution.py:35
  15.8 0.0 collective-permute-done.r1_ref
  15.9 3.5 %collective-permute-done.1.r2_ref = bf16[1024,128]{1,0:T(8,128)(2,1)S(1)} collective-permute-done((bf16[1024,128]{1,0:T(8,128)(2,1)S(1)}, bf16[1024,128]{1,0:T(8,128)(2,1)S(1)}, u32[]{:S(2)}, u32[]{:S(2)}) %collective-permute-start.1) | collective-permute-done | bytes 262176 | tf_op jit(solution)/shard_map/ppermute | solution.py:213
  19.4 0.0 collective-permute-done.2.r3_ref
  19.4 0.8 %pack.2 = (bf16[1056,128]{1,0:T(8,128)(2,1)S(1)}, f32[1024,128]{1,0:T(8,128)S(1)}) custom-call(f32[1024,128]{1,0:T(8,128)S(1)} %get-tuple-element.23.own_ref, bf16[1024,128]{1,0:T(8,128)(2,1)S(1)} %collective-permute-done.r1_ref, bf16[1024,128]{1,0:T(8,128)(2,1)S(1)} %collective-permute-done.1.r2_ref, bf16[1024,128]{1,0:T(8,128)(2,1)S(1)} %collective-permute-done.2.r3_ref, ...), custom_call_target="tpu_custom_call" | custom-call | flops 1073741824 | bytes 2097152 | tf_op jit(solution)/shard_map/pack/pallas_call | solution.py:35
  20.2 0.1 collective-permute-start.3
  20.3 0.8 %pack.3 = bf16[1056,128]{1,0:T(8,128)(2,1)S(1)} custom-call(f32[1024,128]{1,0:T(8,128)S(1)} %get-tuple-element.30.rows_ref, bf16[512,2048]{1,0:T(8,128)(2,1)S(1)} %get-tuple-element.27.place_ref, bf16[2,2048,256]{2,1,0:T(8,128)(2,1)S(1)} %get-tuple-element.28.mask_ref, bf16[64,128]{1,0:T(8,128)(2,1)S(1)} %get-tuple-element.29.meta_ref), custom_call_target="tpu_custom_call" | custom-call | flops 1073741824 | bytes 2097152 | tf_op jit(solution)/shard_map/pack/pallas_call | solution.py:35
  21.1 0.7 %collective-permute-done.3 = bf16[1056,128]{1,0:T(8,128)(2,1)S(1)} collective-permute-done((bf16[1056,128]{1,0:T(8,128)(2,1)S(1)}, bf16[1056,128]{1,0:T(8,128)(2,1)S(1)}, u32[]{:S(2)}, u32[]{:S(2)}) %collective-permute-start.3) | collective-permute-done | bytes 270368 | tf_op jit(solution)/shard_map/ppermute | solution.py:254
  21.9 30.2 %all_to_all.5.msg_ref = bf16[32,72,128]{2,1,0:T(8,128)(2,1)S(1)} all-to-all(bf16[32,72,128]{2,1,0:T(8,128)(2,1)S(1)} %pad_maximum_fusion), channel_id=1, replica_groups={{0,2,4,6,8,10,12,14,16,18,20,22,24,26,28,30,32,34,36,38,40,42,44,46,48,..., dimensions={0} | all-to-all | bytes 1179648 | tf_op jit(solution)/shard_map/all_to_all | solution.py:265
  52.2 1.4 %scatter.1.refs_0_ = bf16[256,128]{1,0:T(8,128)(2,1)S(1)} custom-call(bf16[32,72,128]{2,1,0:T(8,128)(2,1)S(1)} %all_to_all.5.msg_ref), custom_call_target="tpu_custom_call" | custom-call | flops 1073741824 | bytes 2097152 | tf_op jit(solution)/shard_map/scatter/pallas_call | solution.py:35
  53.6 0.1 collective-permute-start.4
  53.7 2.7 %collective-permute-start.5 = (bf16[256,128]{1,0:T(8,128)(2,1)S(1)}, bf16[256,128]{1,0:T(8,128)(2,1)S(1)}, u32[]{:S(2)}, u32[]{:S(2)}) collective-permute-start(bf16[256,128]{1,0:T(8,128)(2,1)S(1)} %scatter.1.refs_0_), channel_id=1, source_target_pairs={{0,128},{1,129},{2,130},{3,131},{4,132},{5,133},{6,134},{7,135},{8... | collective-permute-start | bytes 196616 | tf_op jit(solution)/shard_map/ppermute | solution.py:213
  56.4 1.0 %collective-permute-start.6 = (bf16[256,128]{1,0:T(8,128)(2,1)S(1)}, bf16[256,128]{1,0:T(8,128)(2,1)S(1)}, u32[]{:S(2)}, u32[]{:S(2)}) collective-permute-start(bf16[256,128]{1,0:T(8,128)(2,1)S(1)} %scatter.1.refs_0_), channel_id=1, source_target_pairs={{0,192},{1,65},{2,194},{3,67},{4,196},{5,69},{6,198},{7,71},{8,200... | collective-permute-start | bytes 196616 | tf_op jit(solution)/shard_map/ppermute | solution.py:213
  58.0 1.2 %collective-permute-done.4.refs_1_ = bf16[256,128]{1,0:T(8,128)(2,1)S(1)} collective-permute-done((bf16[256,128]{1,0:T(8,128)(2,1)S(1)}, bf16[256,128]{1,0:T(8,128)(2,1)S(1)}, u32[]{:S(2)}, u32[]{:S(2)}) %collective-permute-start.4) | collective-permute-done | bytes 65568 | tf_op jit(solution)/shard_map/ppermute | solution.py:213
  59.2 0.7 %collective-permute-done.5.refs_2_ = bf16[256,128]{1,0:T(8,128)(2,1)S(1)} collective-permute-done((bf16[256,128]{1,0:T(8,128)(2,1)S(1)}, bf16[256,128]{1,0:T(8,128)(2,1)S(1)}, u32[]{:S(2)}, u32[]{:S(2)}) %collective-permute-start.5) | collective-permute-done | bytes 65568 | tf_op jit(solution)/shard_map/ppermute | solution.py:213
  59.9 0.9 %collective-permute-done.6.refs_3_ = bf16[256,128]{1,0:T(8,128)(2,1)S(1)} collective-permute-done((bf16[256,128]{1,0:T(8,128)(2,1)S(1)}, bf16[256,128]{1,0:T(8,128)(2,1)S(1)}, u32[]{:S(2)}, u32[]{:S(2)}) %collective-permute-start.6) | collective-permute-done | bytes 65568 | tf_op jit(solution)/shard_map/ppermute | solution.py:213
  60.7 1.5 %finish.1 = bf16[1024,256]{1,0:T(8,128)(2,1)} custom-call(s32[1]{0:T(128)S(6)} %copy.8.live_ref, bf16[256,128]{1,0:T(8,128)(2,1)S(1)} %scatter.1.refs_0_, bf16[256,128]{1,0:T(8,128)(2,1)S(1)} %collective-permute-done.4.refs_1_, bf16[256,128]{1,0:T(8,128)(2,1)S(1)} %collective-permute-done.5.refs_2_, bf16[256,128]{1,0:T(8,128)(2,1)S(1)} %collective-permute-done.6.refs_3_, ...), custom_call_target="tpu_custom_call" | custom-call | flops 268435456 | bytes 2097152 | tf_op jit(solution)/shard_map/finish/pallas_call | solution.py:35
  (11 shorter events, 0.1 us)
Async XLA Ops:
  0.0 8.6 %copy-start = (bf16[1,2560,512]{2,1,0:T(8,128)(2,1)S(1)}, bf16[1,2560,512]{2,1,0:T(8,128)(2,1)}, u32[]{:S(2)}) copy-start(bf16[1,2560,512]{2,1,0:T(8,128)(2,1)} %param.11) | copy-start | bytes 7864324
  0.0 1.1 %copy-start.1 = (bf16[512,256]{1,0:T(8,128)(2,1)S(1)}, bf16[512,256]{1,0:T(8,128)(2,1)}, u32[]{:S(2)}) copy-start(bf16[512,256]{1,0:T(8,128)(2,1)} %comb_hbm.1) | copy-start | bytes 786436
  2.6 13.2 %collective-permute-start = (bf16[1024,128]{1,0:T(8,128)(2,1)S(1)}, bf16[1024,128]{1,0:T(8,128)(2,1)S(1)}, u32[]{:S(2)}, u32[]{:S(2)}) collective-permute-start(bf16[1024,128]{1,0:T(8,128)(2,1)S(1)} %get-tuple-element.20), channel_id=1, source_target_pairs={{0,64},{1,193},{2,66},{3,195},{4,68},{5,197},{6,70},{7,199},{8,72}... | collective-permute-start | bytes 786440 | tf_op jit(solution)/shard_map/ppermute | solution.py:213
  4.3 15.1 %collective-permute-start.1 = (bf16[1024,128]{1,0:T(8,128)(2,1)S(1)}, bf16[1024,128]{1,0:T(8,128)(2,1)S(1)}, u32[]{:S(2)}, u32[]{:S(2)}) collective-permute-start(bf16[1024,128]{1,0:T(8,128)(2,1)S(1)} %get-tuple-element.21), channel_id=1, source_target_pairs={{0,128},{1,129},{2,130},{3,131},{4,132},{5,133},{6,134},{7,135},{8... | collective-permute-start | bytes 786440 | tf_op jit(solution)/shard_map/ppermute | solution.py:213
  7.2 6.7 %copy-start.2 = (s32[2048,1]{0,1:T(1,128)S(1)}, s32[2048,1]{0,1:T(1,128)}, u32[]{:S(2)}) copy-start(s32[2048,1]{0,1:T(1,128)} %param.8) | copy-start | bytes 24580
  7.2 6.7 %copy-start.3 = (s32[2048]{0:T(1024)S(1)}, s32[2048]{0:T(1024)}, u32[]{:S(2)}) copy-start(s32[2048]{0:T(1024)} %param.9) | copy-start | bytes 24580
  7.2 12.2 %collective-permute-start.2 = (bf16[1024,128]{1,0:T(8,128)(2,1)S(1)}, bf16[1024,128]{1,0:T(8,128)(2,1)S(1)}, u32[]{:S(2)}, u32[]{:S(2)}) collective-permute-start(bf16[1024,128]{1,0:T(8,128)(2,1)S(1)} %get-tuple-element.22), channel_id=1, source_target_pairs={{0,192},{1,65},{2,194},{3,67},{4,196},{5,69},{6,198},{7,71},{8,200... | collective-permute-start | bytes 786440 | tf_op jit(solution)/shard_map/ppermute | solution.py:213
  20.2 1.6 %collective-permute-start.3 = (bf16[1056,128]{1,0:T(8,128)(2,1)S(1)}, bf16[1056,128]{1,0:T(8,128)(2,1)S(1)}, u32[]{:S(2)}, u32[]{:S(2)}) collective-permute-start(bf16[1056,128]{1,0:T(8,128)(2,1)S(1)} %get-tuple-element.31), channel_id=1, source_target_pairs={{0,1},{1,0},{2,3},{3,2},{4,5},{5,4},{6,7},{7,6},{8,9},{9,8},{10,11... | collective-permute-start | bytes 811016 | tf_op jit(solution)/shard_map/ppermute | solution.py:254
  53.6 5.6 %collective-permute-start.4 = (bf16[256,128]{1,0:T(8,128)(2,1)S(1)}, bf16[256,128]{1,0:T(8,128)(2,1)S(1)}, u32[]{:S(2)}, u32[]{:S(2)}) collective-permute-start(bf16[256,128]{1,0:T(8,128)(2,1)S(1)} %scatter.1.refs_0_), channel_id=1, source_target_pairs={{0,64},{1,193},{2,66},{3,195},{4,68},{5,197},{6,70},{7,199},{8,72}... | collective-permute-start | bytes 196616 | tf_op jit(solution)/shard_map/ppermute | solution.py:213
  53.7 6.2 %collective-permute-start.5 = (bf16[256,128]{1,0:T(8,128)(2,1)S(1)}, bf16[256,128]{1,0:T(8,128)(2,1)S(1)}, u32[]{:S(2)}, u32[]{:S(2)}) collective-permute-start(bf16[256,128]{1,0:T(8,128)(2,1)S(1)} %scatter.1.refs_0_), channel_id=1, source_target_pairs={{0,128},{1,129},{2,130},{3,131},{4,132},{5,133},{6,134},{7,135},{8... | collective-permute-start | bytes 196616 | tf_op jit(solution)/shard_map/ppermute | solution.py:213
  56.4 4.3 %collective-permute-start.6 = (bf16[256,128]{1,0:T(8,128)(2,1)S(1)}, bf16[256,128]{1,0:T(8,128)(2,1)S(1)}, u32[]{:S(2)}, u32[]{:S(2)}) collective-permute-start(bf16[256,128]{1,0:T(8,128)(2,1)S(1)} %scatter.1.refs_0_), channel_id=1, source_target_pairs={{0,192},{1,65},{2,194},{3,67},{4,196},{5,69},{6,198},{7,71},{8,200... | collective-permute-start | bytes 196616 | tf_op jit(solution)/shard_map/ppermute | solution.py:213

commit v4 on v3

--- a/solution.py
+++ b/solution.py
@@ -13,7 +13,7 @@
 GROUP = 16
 MSG = NC * PER + 8
 OUT_PARTS = 4
-FETCH_VMEM = 52
+FETCH_VMEM = 53
 BF, F32 = jnp.bfloat16, jnp.float32
 
 
@@ -42,40 +42,47 @@
     )(*args)
 
 
-def project_kernel(press_hbm, comb_hbm, own_ref, *refs):
+def pieces(first, count, combos):
+    turn = 1 - 2 * (lax.axis_index("se") & 1)
+    source, target = iota((combos, count * LANES), 0), iota((combos, count * LANES), 1)
+    lane = target & (LANES - 1)
+    y = lax.axis_index("case") + turn * ((target >> 7) + first)
+    hit = source == ((y * HALF + (lane & (HALF - 1))) & (combos - 1))
+    return one_hot(hit & (lane < HALF)), one_hot(hit & (lane >= HALF))
+
+
+def product(press, comb, picked):
+    half = press.shape[0] // 2
+    both = jnp.concatenate([press[:half], press[half:]], axis=1)
+    return dot(both, jnp.concatenate([dot(comb, p).astype(BF) for p in picked], axis=0))
+
+
+def case_rows(cases):
+    return pl.ds(pl.multiple_of(lax.axis_index("case") * cases, cases), cases)
+
+
+def project_kernel(press_hbm, comb_hbm, *refs):
     send_refs, (press_ref, comb_ref, sems) = refs[: NY - 1], refs[NY - 1 :]
-    panels, cases = press_ref.shape
-    combos = comb_ref.shape[1]
-    y = lax.axis_index("case")
-    at = pl.ds(pl.multiple_of(y * cases, cases), cases)
-    comb_copy = pltpu.make_async_copy(comb_hbm.at[at], comb_ref, sems.at[0])
+    comb_copy = pltpu.make_async_copy(
+        comb_hbm.at[case_rows(press_ref.shape[1])], comb_ref, sems.at[0]
+    )
     press_copy = pltpu.make_async_copy(press_hbm, press_ref, sems.at[1])
     comb_copy.start()
     press_copy.start()
-    source, target = iota((combos, NY * LANES), 0), iota((combos, NY * LANES), 1)
-    lane = target & (LANES - 1)
-    turn = 1 - 2 * (lax.axis_index("se") & 1)
-    column = ((target >> 7) * (turn * HALF) + (lane & (HALF - 1)) + y * HALF) & (combos - 1)
-    left = one_hot((source == column) & (lane < HALF))
-    right = one_hot((source == column) & (lane >= HALF))
+    picked = pieces(1, NY - 1, comb_ref.shape[1])
     comb_copy.wait()
-    mine = comb_ref[...]
-    first, second = dot(mine, left).astype(BF), dot(mine, right).astype(BF)
     press_copy.wait()
-    half = panels // 2
-    both = jnp.concatenate([press_ref[:half, :], press_ref[half:, :]], axis=1)
-    product = dot(both, jnp.concatenate([first, second], axis=0))
-    own_ref[...] = product[:, :LANES]
+    sent = product(press_ref[...], comb_ref[...], picked)
     for k, ref in enumerate(send_refs):
-        ref[...] = product[:, (k + 1) * LANES : (k + 2) * LANES].astype(BF)
-
-
-def rank_kernel(owner_ref, slot_ref, place_ref, masks_ref, meta_ref):
+        ref[...] = sent[:, k * LANES : (k + 1) * LANES].astype(BF)
+
+
+def rank_kernel(owner_ref, slot_ref, press_ref, comb_ref, place_ref, masks_ref, meta_ref, own_ref):
     panels = owner_ref.shape[1]
     me = lax.axis_index("se")
     owner = owner_ref[...]
     side = (owner ^ me) & 1
-    chip = owner >> 1
+    chip = place_of(owner >> 1, owner & 1)
     owners = CHIPS * NC
     oh = jnp.where(iota((owners, panels), 0) == side * CHIPS + chip, 1.0, 0.0)
     width = 256
@@ -103,6 +110,8 @@
     for s in range(NC):
         for h in range(2):
             masks_ref[s, :, h * LANES : (h + 1) * LANES] = one_hot(groups == part + (s * 4 + h * 2))
+    comb = comb_ref[case_rows(press_ref.shape[1]), :]
+    own_ref[...] = product(press_ref[...], comb, pieces(0, 1, comb.shape[1]))
 
 
 def place_rows(rows, place_ref, mask_ref, meta_ref, out_ref):
@@ -195,11 +204,16 @@
         copy.wait()
 
 
-def se_index(x, z, c):
-    return (x * NZ + z) * NC + c
-
-
-SAME_CORE = [[se_index(x, z, c) for x in range(NX) for z in range(NZ)] for c in range(NC)]
+STRIDE, INVERSE = 7, 23
+
+
+def place_of(chip, core):
+    return (chip * INVERSE + core * (CHIPS // 2)) & (CHIPS - 1)
+
+
+SAME_CORE = [
+    [(place + CHIPS // 2 * c) * STRIDE % CHIPS * NC + c for place in range(CHIPS)] for c in range(NC)
+]
 OTHER_CORE = [(i, i ^ 1) for i in range(NX * NZ * NC)]
 
 
@@ -223,9 +237,9 @@
     panels = panel_press.shape[0]
     points, combos = flexibility.shape[2], combination.shape[1]
     half = panels // 2
-    own, *sent = call(
+    sent = call(
         project_kernel,
-        [shape(half, LANES, dtype=F32)] + [shape(half, LANES)] * (NY - 1),
+        [shape(half, LANES)] * (NY - 1),
         (panel_press, combination),
         1 << 28,
         "project",
@@ -237,11 +251,16 @@
             pltpu.SemaphoreType.DMA((2,)),
         ],
     )
-    parts = [own] + [along_y(sent[k - 1], k) for k in range(1, NY)]
-    place, masks, meta = call(
+    parts = [along_y(sent[k - 1], k) for k in range(1, NY)]
+    place, masks, meta, own = call(
         rank_kernel,
-        (shape(GROUP * PER, panels), shape(NC, panels, 2 * LANES), shape(NC * CHIPS, LANES)),
-        (panel_owner.reshape(1, panels), panel_slot.reshape(1, panels)),
+        (
+            shape(GROUP * PER, panels),
+            shape(NC, panels, 2 * LANES),
+            shape(NC * CHIPS, LANES),
+            shape(half, LANES, dtype=F32),
+        ),
+        (panel_owner.reshape(1, panels), panel_slot.reshape(1, panels), panel_press, combination),
         1 << 28,
         "rank",
     )
@@ -249,7 +268,7 @@
     parts, mat = lax.optimization_barrier((parts, mat))
     packed = shape(CHIPS * PER + CHIPS, LANES)
     theirs, rows = pack(
-        sum_and_pack, 1, parts, place, masks, meta, (packed, shape(half, LANES, dtype=F32))
+        sum_and_pack, 1, [own, *parts], place, masks, meta, (packed, shape(half, LANES, dtype=F32))
     )
     theirs = lax.ppermute(theirs, "se", OTHER_CORE)
     ours = pack(pack_kernel, 0, [rows], place, masks, meta, packed)

time: 62.4 us -> 60.9 us (0.976)
  the two profiles are of different devices: /device:TPU:32 before, /device:TPU:39 now
where the time goes in v4:
time: 60.9 us; the launch traced here: 60.7 us
  blocking collectives  28.9 us (47%)
  waiting for transfers between devices  9.88 us (16%)
  Pallas kernels  8.3 us (14%)
  starting transfers between devices  7.41 us (12%)
  matrix products  5.34 us (9%)
  between operations  0.76 us (1%)
    all_to_all x1, blocking collectives, per_device(): lax.all_to_all(messages, 'se', 0, 0, axis_index_groups=SAME_CORE, tiled=T...  28.9 us
    ppermute x6, waiting for transfers between devices, along_y(): return lax.ppermute(a, ('case', 'se'), pairs)  9.53 us
    pallas_call x6, Pallas kernels, call(): pl.pallas_call(kernel, out_shape=out_shape, compiler_params=pltpu.Compile...  8.3 us
    ppermute x6, starting transfers between devices, along_y(): return lax.ppermute(a, ('case', 'se'), pairs)  5.64 us
    dot_general x1, matrix products, dot(): return jnp.dot(a, b, preferred_element_type=F32)  5.34 us
    ppermute x1, starting transfers between devices, per_device(): theirs = lax.ppermute(theirs, 'se', OTHER_CORE)  1.77 us
  transfers between devices with their start and end apart: 7, of which 6 were waited for; matrix products, arithmetic and copies ran while one was open for 9% of the time, Pallas kernels for 4%

profile of v4, /device:TPU:39, one launch (start us, length us, event | category | flops | bytes accessed | tf_op | source)
XLA Modules:
  0.0 60.7 jit_solution(10284417202109545796)
XLA Ops:
  0.0 0.0 copy-start
  0.0 1.9 %project.1 = (bf16[1024,128]{1,0:T(8,128)(2,1)S(1)}, bf16[1024,128]{1,0:T(8,128)(2,1)S(1)}, bf16[1024,128]{1,0:T(8,128)(2,1)S(1)}) custom-call(bf16[2048,128]{1,0:T(8,128)(2,1)} %press_hbm.1, bf16[512,256]{1,0:T(8,128)(2,1)} %comb_hbm.1), custom_call_target="tpu_custom_call" | custom-call | flops 268435456 | bytes 2097152 | tf_op jit(solution)/shard_map/project/pallas_call | solution.py:35
  1.9 2.8 %collective-permute-start = (bf16[1024,128]{1,0:T(8,128)(2,1)S(1)}, bf16[1024,128]{1,0:T(8,128)(2,1)S(1)}, u32[]{:S(2)}, u32[]{:S(2)}) collective-permute-start(bf16[1024,128]{1,0:T(8,128)(2,1)S(1)} %get-tuple-element.19), channel_id=1, source_target_pairs={{0,64},{1,193},{2,66},{3,195},{4,68},{5,197},{6,70},{7,199},{8,72}... | collective-permute-start | bytes 786440 | tf_op jit(solution)/shard_map/ppermute | solution.py:227
  4.7 0.3 collective-permute-start.1
  5.0 0.8 %collective-permute-start.2 = (bf16[1024,128]{1,0:T(8,128)(2,1)S(1)}, bf16[1024,128]{1,0:T(8,128)(2,1)S(1)}, u32[]{:S(2)}, u32[]{:S(2)}) collective-permute-start(bf16[1024,128]{1,0:T(8,128)(2,1)S(1)} %get-tuple-element.21), channel_id=1, source_target_pairs={{0,192},{1,65},{2,194},{3,67},{4,196},{5,69},{6,198},{7,71},{8,200... | collective-permute-start | bytes 786440 | tf_op jit(solution)/shard_map/ppermute | solution.py:227
  5.8 0.0 copy-done
  5.8 5.3 %fusion.3.refs_4_ = bf16[1024,512]{1,0:T(8,128)(2,1)S(1)} fusion(bf16[1,2560,512]{2,1,0:T(8,128)(2,1)S(1)} %copy-done, bf16[1,1024,2560]{2,1,0:T(8,128)(2,1)} %param.12), kind=kOutput, calls=%fused_computation.3 | convolution fusion | flops 2684878848 | bytes 8912896 | tf_op jit(solution)/shard_map/dot_general | solution.py:29
  11.2 1.9 %rank.1 = (bf16[512,2048]{1,0:T(8,128)(2,1)S(1)}, bf16[2,2048,256]{2,1,0:T(8,128)(2,1)S(1)}, bf16[64,128]{1,0:T(8,128)(2,1)S(1)}, f32[1024,128]{1,0:T(8,128)S(1)}) custom-call(s32[1,2048]{1,0:T(1,128)S(1)} %bitcast.15, s32[1,2048]{1,0:T(1,128)S(1)} %bitcast.16, bf16[2048,128]{1,0:T(8,128)(2,1)S(1)} %copy-done.1, bf16[512,256]{1,0:T(8,128)(2,1)S(1)} %copy-done.2), custom_call_target="tpu_custom_call" | custom-call | flops 268435456 | bytes 2097152 | tf_op jit(solution)/shard_map/rank/pallas_call | solution.py:35
  13.1 1.9 %collective-permute-done.r1_ref = bf16[1024,128]{1,0:T(8,128)(2,1)S(1)} collective-permute-done((bf16[1024,128]{1,0:T(8,128)(2,1)S(1)}, bf16[1024,128]{1,0:T(8,128)(2,1)S(1)}, u32[]{:S(2)}, u32[]{:S(2)}) %collective-permute-start) | collective-permute-done | bytes 262176 | tf_op jit(solution)/shard_map/ppermute | solution.py:227
  15.0 0.0 collective-permute-done.1.r2_ref
  15.0 2.6 %collective-permute-done.2.r3_ref = bf16[1024,128]{1,0:T(8,128)(2,1)S(1)} collective-permute-done((bf16[1024,128]{1,0:T(8,128)(2,1)S(1)}, bf16[1024,128]{1,0:T(8,128)(2,1)S(1)}, u32[]{:S(2)}, u32[]{:S(2)}) %collective-permute-start.2) | collective-permute-done | bytes 262176 | tf_op jit(solution)/shard_map/ppermute | solution.py:227
  17.6 0.8 %pack.2 = (bf16[1056,128]{1,0:T(8,128)(2,1)S(1)}, f32[1024,128]{1,0:T(8,128)S(1)}) custom-call(f32[1024,128]{1,0:T(8,128)S(1)} %get-tuple-element.18.own_ref, bf16[1024,128]{1,0:T(8,128)(2,1)S(1)} %collective-permute-done.r1_ref, bf16[1024,128]{1,0:T(8,128)(2,1)S(1)} %collective-permute-done.1.r2_ref, bf16[1024,128]{1,0:T(8,128)(2,1)S(1)} %collective-permute-done.2.r3_ref, ...), custom_call_target="tpu_custom_call" | custom-call | flops 1073741824 | bytes 2097152 | tf_op jit(solution)/shard_map/pack/pallas_call | solution.py:35
  18.4 1.8 %collective-permute-start.3 = (bf16[1056,128]{1,0:T(8,128)(2,1)S(1)}, bf16[1056,128]{1,0:T(8,128)(2,1)S(1)}, u32[]{:S(2)}, u32[]{:S(2)}) collective-permute-start(bf16[1056,128]{1,0:T(8,128)(2,1)S(1)} %get-tuple-element.29), channel_id=1, source_target_pairs={{0,1},{1,0},{2,3},{3,2},{4,5},{5,4},{6,7},{7,6},{8,9},{9,8},{10,11... | collective-permute-start | bytes 811016 | tf_op jit(solution)/shard_map/ppermute | solution.py:273
  20.2 0.8 %pack.3 = bf16[1056,128]{1,0:T(8,128)(2,1)S(1)} custom-call(f32[1024,128]{1,0:T(8,128)S(1)} %get-tuple-element.28.rows_ref, bf16[512,2048]{1,0:T(8,128)(2,1)S(1)} %get-tuple-element.25.place_ref, bf16[2,2048,256]{2,1,0:T(8,128)(2,1)S(1)} %get-tuple-element.26.mask_ref, bf16[64,128]{1,0:T(8,128)(2,1)S(1)} %get-tuple-element.27.meta_ref), custom_call_target="tpu_custom_call" | custom-call | flops 1073741824 | bytes 2097152 | tf_op jit(solution)/shard_map/pack/pallas_call | solution.py:35
  21.0 0.4 collective-permute-done.3
  21.5 28.9 %all_to_all.5.msg_ref = bf16[32,72,128]{2,1,0:T(8,128)(2,1)S(1)} all-to-all(bf16[32,72,128]{2,1,0:T(8,128)(2,1)S(1)} %pad_maximum_fusion), channel_id=1, replica_groups={{0,14,28,42,56,6,20,34,48,62,12,26,40,54,4,18,32,46,60,10,24,38,52,2,16..., dimensions={0} | all-to-all | bytes 1179648 | tf_op jit(solution)/shard_map/all_to_all | solution.py:284
  50.3 1.4 %scatter.1.refs_0_ = bf16[256,128]{1,0:T(8,128)(2,1)S(1)} custom-call(bf16[32,72,128]{2,1,0:T(8,128)(2,1)S(1)} %all_to_all.5.msg_ref), custom_call_target="tpu_custom_call" | custom-call | flops 1073741824 | bytes 2097152 | tf_op jit(solution)/shard_map/scatter/pallas_call | solution.py:35
  51.8 1.0 %collective-permute-start.4 = (bf16[256,128]{1,0:T(8,128)(2,1)S(1)}, bf16[256,128]{1,0:T(8,128)(2,1)S(1)}, u32[]{:S(2)}, u32[]{:S(2)}) collective-permute-start(bf16[256,128]{1,0:T(8,128)(2,1)S(1)} %scatter.1.refs_0_), channel_id=1, source_target_pairs={{0,64},{1,193},{2,66},{3,195},{4,68},{5,197},{6,70},{7,199},{8,72}... | collective-permute-start | bytes 196616 | tf_op jit(solution)/shard_map/ppermute | solution.py:227
  52.8 0.1 collective-permute-start.5
  52.9 0.6 %collective-permute-start.6 = (bf16[256,128]{1,0:T(8,128)(2,1)S(1)}, bf16[256,128]{1,0:T(8,128)(2,1)S(1)}, u32[]{:S(2)}, u32[]{:S(2)}) collective-permute-start(bf16[256,128]{1,0:T(8,128)(2,1)S(1)} %scatter.1.refs_0_), channel_id=1, source_target_pairs={{0,192},{1,65},{2,194},{3,67},{4,196},{5,69},{6,198},{7,71},{8,200... | collective-permute-start | bytes 196616 | tf_op jit(solution)/shard_map/ppermute | solution.py:227
  54.1 0.8 %collective-permute-done.4.refs_1_ = bf16[256,128]{1,0:T(8,128)(2,1)S(1)} collective-permute-done((bf16[256,128]{1,0:T(8,128)(2,1)S(1)}, bf16[256,128]{1,0:T(8,128)(2,1)S(1)}, u32[]{:S(2)}, u32[]{:S(2)}) %collective-permute-start.4) | collective-permute-done | bytes 65568 | tf_op jit(solution)/shard_map/ppermute | solution.py:227
  55.0 3.4 %collective-permute-done.5.refs_2_ = bf16[256,128]{1,0:T(8,128)(2,1)S(1)} collective-permute-done((bf16[256,128]{1,0:T(8,128)(2,1)S(1)}, bf16[256,128]{1,0:T(8,128)(2,1)S(1)}, u32[]{:S(2)}, u32[]{:S(2)}) %collective-permute-start.5) | collective-permute-done | bytes 65568 | tf_op jit(solution)/shard_map/ppermute | solution.py:227
  58.4 0.8 %collective-permute-done.6.refs_3_ = bf16[256,128]{1,0:T(8,128)(2,1)S(1)} collective-permute-done((bf16[256,128]{1,0:T(8,128)(2,1)S(1)}, bf16[256,128]{1,0:T(8,128)(2,1)S(1)}, u32[]{:S(2)}, u32[]{:S(2)}) %collective-permute-start.6) | collective-permute-done | bytes 65568 | tf_op jit(solution)/shard_map/ppermute | solution.py:227
  59.2 1.5 %finish.1 = bf16[1024,256]{1,0:T(8,128)(2,1)} custom-call(s32[1]{0:T(128)S(6)} %copy.8.live_ref, bf16[256,128]{1,0:T(8,128)(2,1)S(1)} %scatter.1.refs_0_, bf16[256,128]{1,0:T(8,128)(2,1)S(1)} %collective-permute-done.4.refs_1_, bf16[256,128]{1,0:T(8,128)(2,1)S(1)} %collective-permute-done.5.refs_2_, bf16[256,128]{1,0:T(8,128)(2,1)S(1)} %collective-permute-done.6.refs_3_, ...), custom_call_target="tpu_custom_call" | custom-call | flops 268435456 | bytes 2097152 | tf_op jit(solution)/shard_map/finish/pallas_call | solution.py:35
  (13 shorter events, 0.1 us)
Async XLA Ops:
  0.0 5.8 %copy-start = (bf16[1,2560,512]{2,1,0:T(8,128)(2,1)S(1)}, bf16[1,2560,512]{2,1,0:T(8,128)(2,1)}, u32[]{:S(2)}) copy-start(bf16[1,2560,512]{2,1,0:T(8,128)(2,1)} %param.11) | copy-start | bytes 7864324
  1.9 13.1 %collective-permute-start = (bf16[1024,128]{1,0:T(8,128)(2,1)S(1)}, bf16[1024,128]{1,0:T(8,128)(2,1)S(1)}, u32[]{:S(2)}, u32[]{:S(2)}) collective-permute-start(bf16[1024,128]{1,0:T(8,128)(2,1)S(1)} %get-tuple-element.19), channel_id=1, source_target_pairs={{0,64},{1,193},{2,66},{3,195},{4,68},{5,197},{6,70},{7,199},{8,72}... | collective-permute-start | bytes 786440 | tf_op jit(solution)/shard_map/ppermute | solution.py:227
  4.7 10.3 %collective-permute-start.1 = (bf16[1024,128]{1,0:T(8,128)(2,1)S(1)}, bf16[1024,128]{1,0:T(8,128)(2,1)S(1)}, u32[]{:S(2)}, u32[]{:S(2)}) collective-permute-start(bf16[1024,128]{1,0:T(8,128)(2,1)S(1)} %get-tuple-element.20), channel_id=1, source_target_pairs={{0,128},{1,129},{2,130},{3,131},{4,132},{5,133},{6,134},{7,135},{8... | collective-permute-start | bytes 786440 | tf_op jit(solution)/shard_map/ppermute | solution.py:227
  5.0 6.1 %copy-start.1 = (bf16[2048,128]{1,0:T(8,128)(2,1)S(1)}, bf16[2048,128]{1,0:T(8,128)(2,1)}, u32[]{:S(2)}) copy-start(bf16[2048,128]{1,0:T(8,128)(2,1)} %press_hbm.1) | copy-start | bytes 1572868
  5.0 6.1 %copy-start.2 = (bf16[512,256]{1,0:T(8,128)(2,1)S(1)}, bf16[512,256]{1,0:T(8,128)(2,1)}, u32[]{:S(2)}) copy-start(bf16[512,256]{1,0:T(8,128)(2,1)} %comb_hbm.1) | copy-start | bytes 786436
  5.0 6.1 %copy-start.3 = (s32[2048,1]{0,1:T(1,128)S(1)}, s32[2048,1]{0,1:T(1,128)}, u32[]{:S(2)}) copy-start(s32[2048,1]{0,1:T(1,128)} %param.8) | copy-start | bytes 24580
  5.0 6.2 %copy-start.4 = (s32[2048]{0:T(1024)S(1)}, s32[2048]{0:T(1024)}, u32[]{:S(2)}) copy-start(s32[2048]{0:T(1024)} %param.9) | copy-start | bytes 24580
  5.0 12.5 %collective-permute-start.2 = (bf16[1024,128]{1,0:T(8,128)(2,1)S(1)}, bf16[1024,128]{1,0:T(8,128)(2,1)S(1)}, u32[]{:S(2)}, u32[]{:S(2)}) collective-permute-start(bf16[1024,128]{1,0:T(8,128)(2,1)S(1)} %get-tuple-element.21), channel_id=1, source_target_pairs={{0,192},{1,65},{2,194},{3,67},{4,196},{5,69},{6,198},{7,71},{8,200... | collective-permute-start | bytes 786440 | tf_op jit(solution)/shard_map/ppermute | solution.py:227
  18.4 2.9 %collective-permute-start.3 = (bf16[1056,128]{1,0:T(8,128)(2,1)S(1)}, bf16[1056,128]{1,0:T(8,128)(2,1)S(1)}, u32[]{:S(2)}, u32[]{:S(2)}) collective-permute-start(bf16[1056,128]{1,0:T(8,128)(2,1)S(1)} %get-tuple-element.29), channel_id=1, source_target_pairs={{0,1},{1,0},{2,3},{3,2},{4,5},{5,4},{6,7},{7,6},{8,9},{9,8},{10,11... | collective-permute-start | bytes 811016 | tf_op jit(solution)/shard_map/ppermute | solution.py:273
  51.8 3.2 %collective-permute-start.4 = (bf16[256,128]{1,0:T(8,128)(2,1)S(1)}, bf16[256,128]{1,0:T(8,128)(2,1)S(1)}, u32[]{:S(2)}, u32[]{:S(2)}) collective-permute-start(bf16[256,128]{1,0:T(8,128)(2,1)S(1)} %scatter.1.refs_0_), channel_id=1, source_target_pairs={{0,64},{1,193},{2,66},{3,195},{4,68},{5,197},{6,70},{7,199},{8,72}... | collective-permute-start | bytes 196616 | tf_op jit(solution)/shard_map/ppermute | solution.py:227
  52.8 5.6 %collective-permute-start.5 = (bf16[256,128]{1,0:T(8,128)(2,1)S(1)}, bf16[256,128]{1,0:T(8,128)(2,1)S(1)}, u32[]{:S(2)}, u32[]{:S(2)}) collective-permute-start(bf16[256,128]{1,0:T(8,128)(2,1)S(1)} %scatter.1.refs_0_), channel_id=1, source_target_pairs={{0,128},{1,129},{2,130},{3,131},{4,132},{5,133},{6,134},{7,135},{8... | collective-permute-start | bytes 196616 | tf_op jit(solution)/shard_map/ppermute | solution.py:227
  52.9 6.4 %collective-permute-start.6 = (bf16[256,128]{1,0:T(8,128)(2,1)S(1)}, bf16[256,128]{1,0:T(8,128)(2,1)S(1)}, u32[]{:S(2)}, u32[]{:S(2)}) collective-permute-start(bf16[256,128]{1,0:T(8,128)(2,1)S(1)} %scatter.1.refs_0_), channel_id=1, source_target_pairs={{0,192},{1,65},{2,194},{3,67},{4,196},{5,69},{6,198},{7,71},{8,200... | collective-permute-start | bytes 196616 | tf_op jit(solution)/shard_map/ppermute | solution.py:227

commit v5 on v4

--- a/solution.py
+++ b/solution.py
@@ -13,6 +13,7 @@
 GROUP = 16
 MSG = NC * PER + 8
 OUT_PARTS = 4
+FETCHES = 8
 FETCH_VMEM = 53
 BF, F32 = jnp.bfloat16, jnp.float32
 
@@ -51,10 +52,13 @@
     return one_hot(hit & (lane < HALF)), one_hot(hit & (lane >= HALF))
 
 
-def product(press, comb, picked):
+def weights(comb, picked):
+    return jnp.concatenate([dot(comb, p).astype(BF) for p in picked], axis=0)
+
+
+def product(press, weight):
     half = press.shape[0] // 2
-    both = jnp.concatenate([press[:half], press[half:]], axis=1)
-    return dot(both, jnp.concatenate([dot(comb, p).astype(BF) for p in picked], axis=0))
+    return dot(jnp.concatenate([press[:half], press[half:]], axis=1), weight)
 
 
 def case_rows(cases):
@@ -64,15 +68,24 @@
 def project_kernel(press_hbm, comb_hbm, *refs):
     send_refs, (press_ref, comb_ref, sems) = refs[: NY - 1], refs[NY - 1 :]
     comb_copy = pltpu.make_async_copy(
-        comb_hbm.at[case_rows(press_ref.shape[1])], comb_ref, sems.at[0]
-    )
-    press_copy = pltpu.make_async_copy(press_hbm, press_ref, sems.at[1])
+        comb_hbm.at[case_rows(press_ref.shape[1])], comb_ref, sems.at[FETCHES]
+    )
     comb_copy.start()
-    press_copy.start()
+    part = press_ref.shape[0] // FETCHES
+    copies = [
+        pltpu.make_async_copy(
+            press_hbm.at[pl.ds(i * part, part)], press_ref.at[pl.ds(i * part, part)], sems.at[i]
+        )
+        for i in range(FETCHES)
+    ]
+    for copy in copies:
+        copy.start()
     picked = pieces(1, NY - 1, comb_ref.shape[1])
     comb_copy.wait()
-    press_copy.wait()
-    sent = product(press_ref[...], comb_ref[...], picked)
+    weight = weights(comb_ref[...], picked)
+    for copy in copies:
+        copy.wait()
+    sent = product(press_ref[...], weight)
     for k, ref in enumerate(send_refs):
         ref[...] = sent[:, k * LANES : (k + 1) * LANES].astype(BF)
 
@@ -111,7 +124,7 @@
         for h in range(2):
             masks_ref[s, :, h * LANES : (h + 1) * LANES] = one_hot(groups == part + (s * 4 + h * 2))
     comb = comb_ref[case_rows(press_ref.shape[1]), :]
-    own_ref[...] = product(press_ref[...], comb, pieces(0, 1, comb.shape[1]))
+    own_ref[...] = product(press_ref[...], weights(comb, pieces(0, 1, comb.shape[1])))
 
 
 def place_rows(rows, place_ref, mask_ref, meta_ref, out_ref):
@@ -204,16 +217,15 @@
         copy.wait()
 
 
-STRIDE, INVERSE = 7, 23
-
-
 def place_of(chip, core):
-    return (chip * INVERSE + core * (CHIPS // 2)) & (CHIPS - 1)
-
-
-SAME_CORE = [
-    [(place + CHIPS // 2 * c) * STRIDE % CHIPS * NC + c for place in range(CHIPS)] for c in range(NC)
-]
+    return (chip * 5 - 12 * core) & (CHIPS - 1)
+
+
+def chip_at(place, core):
+    return ((place + 12 * core) * 13) & (CHIPS - 1)
+
+
+SAME_CORE = [[chip_at(place, c) * NC + c for place in range(CHIPS)] for c in range(NC)]
 OTHER_CORE = [(i, i ^ 1) for i in range(NX * NZ * NC)]
 
 
@@ -248,7 +260,7 @@
         scratch_shapes=[
             pltpu.VMEM(panel_press.shape, BF),
             pltpu.VMEM((panel_press.shape[1], combos), BF),
-            pltpu.SemaphoreType.DMA((2,)),
+            pltpu.SemaphoreType.DMA((FETCHES + 1,)),
         ],
     )
     parts = [along_y(sent[k - 1], k) for k in range(1, NY)]

time: 60.9 us -> 59.1 us (0.970)
  the two profiles are of different devices: /device:TPU:39 before, /device:TPU:32 now
where the time goes in v5:
time: 59.1 us; the launch traced here: 58.9 us
  blocking collectives  27.6 us (47%)
  starting transfers between devices  9.83 us (17%)
  Pallas kernels  8.22 us (14%)
  waiting for transfers between devices  7 us (12%)
  matrix products  5.34 us (9%)
  between operations  0.79 us (1%)
    all_to_all x1, blocking collectives, per_device(): lax.all_to_all(messages, 'se', 0, 0, axis_index_groups=SAME_CORE, tiled=T...  27.6 us
    ppermute x6, starting transfers between devices, along_y(): return lax.ppermute(a, ('case', 'se'), pairs)  9.74 us
    pallas_call x6, Pallas kernels, call(): pl.pallas_call(kernel, out_shape=out_shape, compiler_params=pltpu.Compile...  8.22 us
    ppermute x6, waiting for transfers between devices, along_y(): return lax.ppermute(a, ('case', 'se'), pairs)  6.28 us
    dot_general x1, matrix products, dot(): return jnp.dot(a, b, preferred_element_type=F32)  5.34 us
  transfers between devices with their start and end apart: 7, of which 3 were waited for; matrix products, arithmetic and copies ran while one was open for 9% of the time, Pallas kernels for 5%

profile of v5, /device:TPU:32, one launch (start us, length us, event | category | flops | bytes accessed | tf_op | source)
XLA Modules:
  0.0 58.9 jit_solution(8516603933954334855)
XLA Ops:
  0.0 0.0 copy-start
  0.0 1.8 %project.1 = (bf16[1024,128]{1,0:T(8,128)(2,1)S(1)}, bf16[1024,128]{1,0:T(8,128)(2,1)S(1)}, bf16[1024,128]{1,0:T(8,128)(2,1)S(1)}) custom-call(bf16[2048,128]{1,0:T(8,128)(2,1)} %press_hbm.1, bf16[512,256]{1,0:T(8,128)(2,1)} %comb_hbm.1), custom_call_target="tpu_custom_call" | custom-call | flops 268435456 | bytes 2097152 | tf_op jit(solution)/shard_map/project/pallas_call | solution.py:36
  1.8 1.7 %collective-permute-start = (bf16[1024,128]{1,0:T(8,128)(2,1)S(1)}, bf16[1024,128]{1,0:T(8,128)(2,1)S(1)}, u32[]{:S(2)}, u32[]{:S(2)}) collective-permute-start(bf16[1024,128]{1,0:T(8,128)(2,1)S(1)} %get-tuple-element.19), channel_id=1, source_target_pairs={{0,64},{1,193},{2,66},{3,195},{4,68},{5,197},{6,70},{7,199},{8,72}... | collective-permute-start | bytes 786440 | tf_op jit(solution)/shard_map/ppermute | solution.py:239
  3.4 2.9 %collective-permute-start.1 = (bf16[1024,128]{1,0:T(8,128)(2,1)S(1)}, bf16[1024,128]{1,0:T(8,128)(2,1)S(1)}, u32[]{:S(2)}, u32[]{:S(2)}) collective-permute-start(bf16[1024,128]{1,0:T(8,128)(2,1)S(1)} %get-tuple-element.20), channel_id=1, source_target_pairs={{0,128},{1,129},{2,130},{3,131},{4,132},{5,133},{6,134},{7,135},{8... | collective-permute-start | bytes 786440 | tf_op jit(solution)/shard_map/ppermute | solution.py:239
  6.4 1.4 %collective-permute-start.2 = (bf16[1024,128]{1,0:T(8,128)(2,1)S(1)}, bf16[1024,128]{1,0:T(8,128)(2,1)S(1)}, u32[]{:S(2)}, u32[]{:S(2)}) collective-permute-start(bf16[1024,128]{1,0:T(8,128)(2,1)S(1)} %get-tuple-element.21), channel_id=1, source_target_pairs={{0,192},{1,65},{2,194},{3,67},{4,196},{5,69},{6,198},{7,71},{8,200... | collective-permute-start | bytes 786440 | tf_op jit(solution)/shard_map/ppermute | solution.py:239
  7.8 0.0 copy-done
  7.8 5.3 %fusion.3.refs_4_ = bf16[1024,512]{1,0:T(8,128)(2,1)S(1)} fusion(bf16[1,2560,512]{2,1,0:T(8,128)(2,1)S(1)} %copy-done, bf16[1,1024,2560]{2,1,0:T(8,128)(2,1)} %param.12), kind=kOutput, calls=%fused_computation.3 | convolution fusion | flops 2684878848 | bytes 8912896 | tf_op jit(solution)/shard_map/dot_general | solution.py:30
  13.2 1.9 %rank.1 = (bf16[512,2048]{1,0:T(8,128)(2,1)S(1)}, bf16[2,2048,256]{2,1,0:T(8,128)(2,1)S(1)}, bf16[64,128]{1,0:T(8,128)(2,1)S(1)}, f32[1024,128]{1,0:T(8,128)S(1)}) custom-call(s32[1,2048]{1,0:T(1,128)S(1)} %bitcast.15, s32[1,2048]{1,0:T(1,128)S(1)} %bitcast.16, bf16[2048,128]{1,0:T(8,128)(2,1)S(1)} %copy-done.1, bf16[512,256]{1,0:T(8,128)(2,1)S(1)} %copy-done.2), custom_call_target="tpu_custom_call" | custom-call | flops 268435456 | bytes 2097152 | tf_op jit(solution)/shard_map/rank/pallas_call | solution.py:36
  15.1 0.0 collective-permute-done.r1_ref
  15.1 3.4 %collective-permute-done.1.r2_ref = bf16[1024,128]{1,0:T(8,128)(2,1)S(1)} collective-permute-done((bf16[1024,128]{1,0:T(8,128)(2,1)S(1)}, bf16[1024,128]{1,0:T(8,128)(2,1)S(1)}, u32[]{:S(2)}, u32[]{:S(2)}) %collective-permute-start.1) | collective-permute-done | bytes 262176 | tf_op jit(solution)/shard_map/ppermute | solution.py:239
  18.5 0.0 collective-permute-done.2.r3_ref
  18.5 0.8 %pack.2 = (bf16[1056,128]{1,0:T(8,128)(2,1)S(1)}, f32[1024,128]{1,0:T(8,128)S(1)}) custom-call(f32[1024,128]{1,0:T(8,128)S(1)} %get-tuple-element.18.own_ref, bf16[1024,128]{1,0:T(8,128)(2,1)S(1)} %collective-permute-done.r1_ref, bf16[1024,128]{1,0:T(8,128)(2,1)S(1)} %collective-permute-done.1.r2_ref, bf16[1024,128]{1,0:T(8,128)(2,1)S(1)} %collective-permute-done.2.r3_ref, ...), custom_call_target="tpu_custom_call" | custom-call | flops 1073741824 | bytes 2097152 | tf_op jit(solution)/shard_map/pack/pallas_call | solution.py:36
  19.3 0.1 collective-permute-start.3
  19.4 0.8 %pack.3 = bf16[1056,128]{1,0:T(8,128)(2,1)S(1)} custom-call(f32[1024,128]{1,0:T(8,128)S(1)} %get-tuple-element.28.rows_ref, bf16[512,2048]{1,0:T(8,128)(2,1)S(1)} %get-tuple-element.25.place_ref, bf16[2,2048,256]{2,1,0:T(8,128)(2,1)S(1)} %get-tuple-element.26.mask_ref, bf16[64,128]{1,0:T(8,128)(2,1)S(1)} %get-tuple-element.27.meta_ref), custom_call_target="tpu_custom_call" | custom-call | flops 1073741824 | bytes 2097152 | tf_op jit(solution)/shard_map/pack/pallas_call | solution.py:36
  20.3 0.7 %collective-permute-done.3 = bf16[1056,128]{1,0:T(8,128)(2,1)S(1)} collective-permute-done((bf16[1056,128]{1,0:T(8,128)(2,1)S(1)}, bf16[1056,128]{1,0:T(8,128)(2,1)S(1)}, u32[]{:S(2)}, u32[]{:S(2)}) %collective-permute-start.3) | collective-permute-done | bytes 270368 | tf_op jit(solution)/shard_map/ppermute | solution.py:285
  21.1 27.6 %all_to_all.5.msg_ref = bf16[32,72,128]{2,1,0:T(8,128)(2,1)S(1)} all-to-all(bf16[32,72,128]{2,1,0:T(8,128)(2,1)S(1)} %pad_maximum_fusion), channel_id=1, replica_groups={{0,26,52,14,40,2,28,54,16,42,4,30,56,18,44,6,32,58,20,46,8,34,60,22,48,..., dimensions={0} | all-to-all | bytes 1179648 | tf_op jit(solution)/shard_map/all_to_all | solution.py:296
  48.7 1.4 %scatter.1.refs_0_ = bf16[256,128]{1,0:T(8,128)(2,1)S(1)} custom-call(bf16[32,72,128]{2,1,0:T(8,128)(2,1)S(1)} %all_to_all.5.msg_ref), custom_call_target="tpu_custom_call" | custom-call | flops 1073741824 | bytes 2097152 | tf_op jit(solution)/shard_map/scatter/pallas_call | solution.py:36
  50.1 0.1 collective-permute-start.4
  50.2 2.7 %collective-permute-start.5 = (bf16[256,128]{1,0:T(8,128)(2,1)S(1)}, bf16[256,128]{1,0:T(8,128)(2,1)S(1)}, u32[]{:S(2)}, u32[]{:S(2)}) collective-permute-start(bf16[256,128]{1,0:T(8,128)(2,1)S(1)} %scatter.1.refs_0_), channel_id=1, source_target_pairs={{0,128},{1,129},{2,130},{3,131},{4,132},{5,133},{6,134},{7,135},{8... | collective-permute-start | bytes 196616 | tf_op jit(solution)/shard_map/ppermute | solution.py:239
  52.9 1.0 %collective-permute-start.6 = (bf16[256,128]{1,0:T(8,128)(2,1)S(1)}, bf16[256,128]{1,0:T(8,128)(2,1)S(1)}, u32[]{:S(2)}, u32[]{:S(2)}) collective-permute-start(bf16[256,128]{1,0:T(8,128)(2,1)S(1)} %scatter.1.refs_0_), channel_id=1, source_target_pairs={{0,192},{1,65},{2,194},{3,67},{4,196},{5,69},{6,198},{7,71},{8,200... | collective-permute-start | bytes 196616 | tf_op jit(solution)/shard_map/ppermute | solution.py:239
  54.6 2.9 %collective-permute-done.4.refs_1_ = bf16[256,128]{1,0:T(8,128)(2,1)S(1)} collective-permute-done((bf16[256,128]{1,0:T(8,128)(2,1)S(1)}, bf16[256,128]{1,0:T(8,128)(2,1)S(1)}, u32[]{:S(2)}, u32[]{:S(2)}) %collective-permute-start.4) | collective-permute-done | bytes 65568 | tf_op jit(solution)/shard_map/ppermute | solution.py:239
  57.5 0.0 collective-permute-done.5.refs_2_
  57.5 0.0 collective-permute-done.6.refs_3_
  57.5 1.5 %finish.1 = bf16[1024,256]{1,0:T(8,128)(2,1)} custom-call(s32[1]{0:T(128)S(6)} %copy.8.live_ref, bf16[256,128]{1,0:T(8,128)(2,1)S(1)} %scatter.1.refs_0_, bf16[256,128]{1,0:T(8,128)(2,1)S(1)} %collective-permute-done.4.refs_1_, bf16[256,128]{1,0:T(8,128)(2,1)S(1)} %collective-permute-done.5.refs_2_, bf16[256,128]{1,0:T(8,128)(2,1)S(1)} %collective-permute-done.6.refs_3_, ...), custom_call_target="tpu_custom_call" | custom-call | flops 268435456 | bytes 2097152 | tf_op jit(solution)/shard_map/finish/pallas_call | solution.py:36
  (13 shorter events, 0.1 us)
Async XLA Ops:
  0.0 7.8 %copy-start = (bf16[1,2560,512]{2,1,0:T(8,128)(2,1)S(1)}, bf16[1,2560,512]{2,1,0:T(8,128)(2,1)}, u32[]{:S(2)}) copy-start(bf16[1,2560,512]{2,1,0:T(8,128)(2,1)} %param.11) | copy-start | bytes 7864324
  1.8 13.3 %collective-permute-start = (bf16[1024,128]{1,0:T(8,128)(2,1)S(1)}, bf16[1024,128]{1,0:T(8,128)(2,1)S(1)}, u32[]{:S(2)}, u32[]{:S(2)}) collective-permute-start(bf16[1024,128]{1,0:T(8,128)(2,1)S(1)} %get-tuple-element.19), channel_id=1, source_target_pairs={{0,64},{1,193},{2,66},{3,195},{4,68},{5,197},{6,70},{7,199},{8,72}... | collective-permute-start | bytes 786440 | tf_op jit(solution)/shard_map/ppermute | solution.py:239
  3.4 15.1 %collective-permute-start.1 = (bf16[1024,128]{1,0:T(8,128)(2,1)S(1)}, bf16[1024,128]{1,0:T(8,128)(2,1)S(1)}, u32[]{:S(2)}, u32[]{:S(2)}) collective-permute-start(bf16[1024,128]{1,0:T(8,128)(2,1)S(1)} %get-tuple-element.20), channel_id=1, source_target_pairs={{0,128},{1,129},{2,130},{3,131},{4,132},{5,133},{6,134},{7,135},{8... | collective-permute-start | bytes 786440 | tf_op jit(solution)/shard_map/ppermute | solution.py:239
  6.3 6.8 %copy-start.1 = (bf16[2048,128]{1,0:T(8,128)(2,1)S(1)}, bf16[2048,128]{1,0:T(8,128)(2,1)}, u32[]{:S(2)}) copy-start(bf16[2048,128]{1,0:T(8,128)(2,1)} %press_hbm.1) | copy-start | bytes 1572868
  6.3 6.8 %copy-start.2 = (bf16[512,256]{1,0:T(8,128)(2,1)S(1)}, bf16[512,256]{1,0:T(8,128)(2,1)}, u32[]{:S(2)}) copy-start(bf16[512,256]{1,0:T(8,128)(2,1)} %comb_hbm.1) | copy-start | bytes 786436
  6.3 6.8 %copy-start.3 = (s32[2048,1]{0,1:T(1,128)S(1)}, s32[2048,1]{0,1:T(1,128)}, u32[]{:S(2)}) copy-start(s32[2048,1]{0,1:T(1,128)} %param.8) | copy-start | bytes 24580
  6.3 6.8 %copy-start.4 = (s32[2048]{0:T(1024)S(1)}, s32[2048]{0:T(1024)}, u32[]{:S(2)}) copy-start(s32[2048]{0:T(1024)} %param.9) | copy-start | bytes 24580
  6.4 12.2 %collective-permute-start.2 = (bf16[1024,128]{1,0:T(8,128)(2,1)S(1)}, bf16[1024,128]{1,0:T(8,128)(2,1)S(1)}, u32[]{:S(2)}, u32[]{:S(2)}) collective-permute-start(bf16[1024,128]{1,0:T(8,128)(2,1)S(1)} %get-tuple-element.21), channel_id=1, source_target_pairs={{0,192},{1,65},{2,194},{3,67},{4,196},{5,69},{6,198},{7,71},{8,200... | collective-permute-start | bytes 786440 | tf_op jit(solution)/shard_map/ppermute | solution.py:239
  19.3 1.6 %collective-permute-start.3 = (bf16[1056,128]{1,0:T(8,128)(2,1)S(1)}, bf16[1056,128]{1,0:T(8,128)(2,1)S(1)}, u32[]{:S(2)}, u32[]{:S(2)}) collective-permute-start(bf16[1056,128]{1,0:T(8,128)(2,1)S(1)} %get-tuple-element.29), channel_id=1, source_target_pairs={{0,1},{1,0},{2,3},{3,2},{4,5},{5,4},{6,7},{7,6},{8,9},{9,8},{10,11... | collective-permute-start | bytes 811016 | tf_op jit(solution)/shard_map/ppermute | solution.py:285
  50.1 7.3 %collective-permute-start.4 = (bf16[256,128]{1,0:T(8,128)(2,1)S(1)}, bf16[256,128]{1,0:T(8,128)(2,1)S(1)}, u32[]{:S(2)}, u32[]{:S(2)}) collective-permute-start(bf16[256,128]{1,0:T(8,128)(2,1)S(1)} %scatter.1.refs_0_), channel_id=1, source_target_pairs={{0,64},{1,193},{2,66},{3,195},{4,68},{5,197},{6,70},{7,199},{8,72}... | collective-permute-start | bytes 196616 | tf_op jit(solution)/shard_map/ppermute | solution.py:239
  50.2 7.2 %collective-permute-start.5 = (bf16[256,128]{1,0:T(8,128)(2,1)S(1)}, bf16[256,128]{1,0:T(8,128)(2,1)S(1)}, u32[]{:S(2)}, u32[]{:S(2)}) collective-permute-start(bf16[256,128]{1,0:T(8,128)(2,1)S(1)} %scatter.1.refs_0_), channel_id=1, source_target_pairs={{0,128},{1,129},{2,130},{3,131},{4,132},{5,133},{6,134},{7,135},{8... | collective-permute-start | bytes 196616 | tf_op jit(solution)/shard_map/ppermute | solution.py:239
  52.9 4.5 %collective-permute-start.6 = (bf16[256,128]{1,0:T(8,128)(2,1)S(1)}, bf16[256,128]{1,0:T(8,128)(2,1)S(1)}, u32[]{:S(2)}, u32[]{:S(2)}) collective-permute-start(bf16[256,128]{1,0:T(8,128)(2,1)S(1)} %scatter.1.refs_0_), channel_id=1, source_target_pairs={{0,192},{1,65},{2,194},{3,67},{4,196},{5,69},{6,198},{7,71},{8,200... | collective-permute-start | bytes 196616 | tf_op jit(solution)/shard_map/ppermute | solution.py:239

commit v6 on v5

--- a/solution.py
+++ b/solution.py
@@ -218,14 +218,12 @@
 
 
 def place_of(chip, core):
-    return (chip * 5 - 12 * core) & (CHIPS - 1)
-
-
-def chip_at(place, core):
-    return ((place + 12 * core) * 13) & (CHIPS - 1)
-
-
-SAME_CORE = [[chip_at(place, c) * NC + c for place in range(CHIPS)] for c in range(NC)]
+    return (((chip & 7) * 4 + (chip >> 3)) * 13 - 12 * core) & (CHIPS - 1)
+
+
+SAME_CORE = [
+    [chip * NC + c for chip in sorted(range(CHIPS), key=lambda chip: place_of(chip, c))] for c in range(NC)
+]
 OTHER_CORE = [(i, i ^ 1) for i in range(NX * NZ * NC)]
 
 

time: 59.1 us -> 58.7 us (level)
  transfers between devices with their start and end apart: 7 -> 7, of which waited for: 3 -> 4; matrix products, arithmetic and copies ran while one was open for 9% -> 9% of each run, Pallas kernels for 5% -> 5%
where the time goes in v6:
time: 58.7 us; the launch traced here: 58.4 us
  blocking collectives  27.3 us (47%)
  starting transfers between devices  9.76 us (17%)
  Pallas kernels  8.22 us (14%)
  waiting for transfers between devices  6.86 us (12%)
  matrix products  5.34 us (9%)
  between operations  0.79 us (1%)
    all_to_all x1, blocking collectives, per_device(): lax.all_to_all(messages, 'se', 0, 0, axis_index_groups=SAME_CORE, tiled=T...  27.3 us
    ppermute x6, starting transfers between devices, along_y(): return lax.ppermute(a, ('case', 'se'), pairs)  9.67 us
    pallas_call x6, Pallas kernels, call(): pl.pallas_call(kernel, out_shape=out_shape, compiler_params=pltpu.Compile...  8.22 us
    ppermute x6, waiting for transfers between devices, along_y(): return lax.ppermute(a, ('case', 'se'), pairs)  6.14 us
    dot_general x1, matrix products, dot(): return jnp.dot(a, b, preferred_element_type=F32)  5.34 us
  transfers between devices with their start and end apart: 7, of which 4 were waited for; matrix products, arithmetic and copies ran while one was open for 9% of the time, Pallas kernels for 5%

profile of v6, /device:TPU:32, one launch (start us, length us, event | category | flops | bytes accessed | tf_op | source)
XLA Modules:
  0.0 58.4 jit_solution(1975766205905254971)
XLA Ops:
  0.0 0.0 copy-start
  0.0 1.8 %project.1 = (bf16[1024,128]{1,0:T(8,128)(2,1)S(1)}, bf16[1024,128]{1,0:T(8,128)(2,1)S(1)}, bf16[1024,128]{1,0:T(8,128)(2,1)S(1)}) custom-call(bf16[2048,128]{1,0:T(8,128)(2,1)} %press_hbm.1, bf16[512,256]{1,0:T(8,128)(2,1)} %comb_hbm.1), custom_call_target="tpu_custom_call" | custom-call | flops 268435456 | bytes 2097152 | tf_op jit(solution)/shard_map/project/pallas_call | solution.py:36
  1.8 1.7 %collective-permute-start = (bf16[1024,128]{1,0:T(8,128)(2,1)S(1)}, bf16[1024,128]{1,0:T(8,128)(2,1)S(1)}, u32[]{:S(2)}, u32[]{:S(2)}) collective-permute-start(bf16[1024,128]{1,0:T(8,128)(2,1)S(1)} %get-tuple-element.19), channel_id=1, source_target_pairs={{0,64},{1,193},{2,66},{3,195},{4,68},{5,197},{6,70},{7,199},{8,72}... | collective-permute-start | bytes 786440 | tf_op jit(solution)/shard_map/ppermute | solution.py:237
  3.4 2.9 %collective-permute-start.1 = (bf16[1024,128]{1,0:T(8,128)(2,1)S(1)}, bf16[1024,128]{1,0:T(8,128)(2,1)S(1)}, u32[]{:S(2)}, u32[]{:S(2)}) collective-permute-start(bf16[1024,128]{1,0:T(8,128)(2,1)S(1)} %get-tuple-element.20), channel_id=1, source_target_pairs={{0,128},{1,129},{2,130},{3,131},{4,132},{5,133},{6,134},{7,135},{8... | collective-permute-start | bytes 786440 | tf_op jit(solution)/shard_map/ppermute | solution.py:237
  6.4 1.4 %collective-permute-start.2 = (bf16[1024,128]{1,0:T(8,128)(2,1)S(1)}, bf16[1024,128]{1,0:T(8,128)(2,1)S(1)}, u32[]{:S(2)}, u32[]{:S(2)}) collective-permute-start(bf16[1024,128]{1,0:T(8,128)(2,1)S(1)} %get-tuple-element.21), channel_id=1, source_target_pairs={{0,192},{1,65},{2,194},{3,67},{4,196},{5,69},{6,198},{7,71},{8,200... | collective-permute-start | bytes 786440 | tf_op jit(solution)/shard_map/ppermute | solution.py:237
  7.8 0.0 copy-done
  7.8 5.3 %fusion.3.refs_4_ = bf16[1024,512]{1,0:T(8,128)(2,1)S(1)} fusion(bf16[1,2560,512]{2,1,0:T(8,128)(2,1)S(1)} %copy-done, bf16[1,1024,2560]{2,1,0:T(8,128)(2,1)} %param.12), kind=kOutput, calls=%fused_computation.3 | convolution fusion | flops 2684878848 | bytes 8912896 | tf_op jit(solution)/shard_map/dot_general | solution.py:30
  13.2 1.9 %rank.1 = (bf16[512,2048]{1,0:T(8,128)(2,1)S(1)}, bf16[2,2048,256]{2,1,0:T(8,128)(2,1)S(1)}, bf16[64,128]{1,0:T(8,128)(2,1)S(1)}, f32[1024,128]{1,0:T(8,128)S(1)}) custom-call(s32[1,2048]{1,0:T(1,128)S(1)} %bitcast.15, s32[1,2048]{1,0:T(1,128)S(1)} %bitcast.16, bf16[2048,128]{1,0:T(8,128)(2,1)S(1)} %copy-done.1, bf16[512,256]{1,0:T(8,128)(2,1)S(1)} %copy-done.2), custom_call_target="tpu_custom_call" | custom-call | flops 268435456 | bytes 2097152 | tf_op jit(solution)/shard_map/rank/pallas_call | solution.py:36
  15.1 0.0 collective-permute-done.r1_ref
  15.1 3.4 %collective-permute-done.1.r2_ref = bf16[1024,128]{1,0:T(8,128)(2,1)S(1)} collective-permute-done((bf16[1024,128]{1,0:T(8,128)(2,1)S(1)}, bf16[1024,128]{1,0:T(8,128)(2,1)S(1)}, u32[]{:S(2)}, u32[]{:S(2)}) %collective-permute-start.1) | collective-permute-done | bytes 262176 | tf_op jit(solution)/shard_map/ppermute | solution.py:237
  18.5 0.0 collective-permute-done.2.r3_ref
  18.5 0.8 %pack.2 = (bf16[1056,128]{1,0:T(8,128)(2,1)S(1)}, f32[1024,128]{1,0:T(8,128)S(1)}) custom-call(f32[1024,128]{1,0:T(8,128)S(1)} %get-tuple-element.18.own_ref, bf16[1024,128]{1,0:T(8,128)(2,1)S(1)} %collective-permute-done.r1_ref, bf16[1024,128]{1,0:T(8,128)(2,1)S(1)} %collective-permute-done.1.r2_ref, bf16[1024,128]{1,0:T(8,128)(2,1)S(1)} %collective-permute-done.2.r3_ref, ...), custom_call_target="tpu_custom_call" | custom-call | flops 1073741824 | bytes 2097152 | tf_op jit(solution)/shard_map/pack/pallas_call | solution.py:36
  19.3 0.1 collective-permute-start.3
  19.4 0.8 %pack.3 = bf16[1056,128]{1,0:T(8,128)(2,1)S(1)} custom-call(f32[1024,128]{1,0:T(8,128)S(1)} %get-tuple-element.28.rows_ref, bf16[512,2048]{1,0:T(8,128)(2,1)S(1)} %get-tuple-element.25.place_ref, bf16[2,2048,256]{2,1,0:T(8,128)(2,1)S(1)} %get-tuple-element.26.mask_ref, bf16[64,128]{1,0:T(8,128)(2,1)S(1)} %get-tuple-element.27.meta_ref), custom_call_target="tpu_custom_call" | custom-call | flops 1073741824 | bytes 2097152 | tf_op jit(solution)/shard_map/pack/pallas_call | solution.py:36
  20.3 0.7 %collective-permute-done.3 = bf16[1056,128]{1,0:T(8,128)(2,1)S(1)} collective-permute-done((bf16[1056,128]{1,0:T(8,128)(2,1)S(1)}, bf16[1056,128]{1,0:T(8,128)(2,1)S(1)}, u32[]{:S(2)}, u32[]{:S(2)}) %collective-permute-start.3) | collective-permute-done | bytes 270368 | tf_op jit(solution)/shard_map/ppermute | solution.py:283
  21.1 27.3 %all_to_all.5.msg_ref = bf16[32,72,128]{2,1,0:T(8,128)(2,1)S(1)} all-to-all(bf16[32,72,128]{2,1,0:T(8,128)(2,1)S(1)} %pad_maximum_fusion), channel_id=1, replica_groups={{0,18,36,54,10,28,46,48,4,22,40,58,14,16,34,52,8,26,44,62,2,20,38,56,12..., dimensions={0} | all-to-all | bytes 1179648 | tf_op jit(solution)/shard_map/all_to_all | solution.py:294
  48.3 1.4 %scatter.1.refs_0_ = bf16[256,128]{1,0:T(8,128)(2,1)S(1)} custom-call(bf16[32,72,128]{2,1,0:T(8,128)(2,1)S(1)} %all_to_all.5.msg_ref), custom_call_target="tpu_custom_call" | custom-call | flops 1073741824 | bytes 2097152 | tf_op jit(solution)/shard_map/scatter/pallas_call | solution.py:36
  49.8 0.1 collective-permute-start.4
  49.9 2.7 %collective-permute-start.5 = (bf16[256,128]{1,0:T(8,128)(2,1)S(1)}, bf16[256,128]{1,0:T(8,128)(2,1)S(1)}, u32[]{:S(2)}, u32[]{:S(2)}) collective-permute-start(bf16[256,128]{1,0:T(8,128)(2,1)S(1)} %scatter.1.refs_0_), channel_id=1, source_target_pairs={{0,128},{1,129},{2,130},{3,131},{4,132},{5,133},{6,134},{7,135},{8... | collective-permute-start | bytes 196616 | tf_op jit(solution)/shard_map/ppermute | solution.py:237
  52.6 0.9 %collective-permute-start.6 = (bf16[256,128]{1,0:T(8,128)(2,1)S(1)}, bf16[256,128]{1,0:T(8,128)(2,1)S(1)}, u32[]{:S(2)}, u32[]{:S(2)}) collective-permute-start(bf16[256,128]{1,0:T(8,128)(2,1)S(1)} %scatter.1.refs_0_), channel_id=1, source_target_pairs={{0,192},{1,65},{2,194},{3,67},{4,196},{5,69},{6,198},{7,71},{8,200... | collective-permute-start | bytes 196616 | tf_op jit(solution)/shard_map/ppermute | solution.py:237
  54.1 1.9 %collective-permute-done.4.refs_1_ = bf16[256,128]{1,0:T(8,128)(2,1)S(1)} collective-permute-done((bf16[256,128]{1,0:T(8,128)(2,1)S(1)}, bf16[256,128]{1,0:T(8,128)(2,1)S(1)}, u32[]{:S(2)}, u32[]{:S(2)}) %collective-permute-start.4) | collective-permute-done | bytes 65568 | tf_op jit(solution)/shard_map/ppermute | solution.py:237
  56.0 0.0 collective-permute-done.5.refs_2_
  56.0 0.9 %collective-permute-done.6.refs_3_ = bf16[256,128]{1,0:T(8,128)(2,1)S(1)} collective-permute-done((bf16[256,128]{1,0:T(8,128)(2,1)S(1)}, bf16[256,128]{1,0:T(8,128)(2,1)S(1)}, u32[]{:S(2)}, u32[]{:S(2)}) %collective-permute-start.6) | collective-permute-done | bytes 65568 | tf_op jit(solution)/shard_map/ppermute | solution.py:237
  56.9 1.5 %finish.1 = bf16[1024,256]{1,0:T(8,128)(2,1)} custom-call(s32[1]{0:T(128)S(6)} %copy.8.live_ref, bf16[256,128]{1,0:T(8,128)(2,1)S(1)} %scatter.1.refs_0_, bf16[256,128]{1,0:T(8,128)(2,1)S(1)} %collective-permute-done.4.refs_1_, bf16[256,128]{1,0:T(8,128)(2,1)S(1)} %collective-permute-done.5.refs_2_, bf16[256,128]{1,0:T(8,128)(2,1)S(1)} %collective-permute-done.6.refs_3_, ...), custom_call_target="tpu_custom_call" | custom-call | flops 268435456 | bytes 2097152 | tf_op jit(solution)/shard_map/finish/pallas_call | solution.py:36
  (13 shorter events, 0.1 us)
Async XLA Ops:
  0.0 7.8 %copy-start = (bf16[1,2560,512]{2,1,0:T(8,128)(2,1)S(1)}, bf16[1,2560,512]{2,1,0:T(8,128)(2,1)}, u32[]{:S(2)}) copy-start(bf16[1,2560,512]{2,1,0:T(8,128)(2,1)} %param.11) | copy-start | bytes 7864324
  1.8 13.3 %collective-permute-start = (bf16[1024,128]{1,0:T(8,128)(2,1)S(1)}, bf16[1024,128]{1,0:T(8,128)(2,1)S(1)}, u32[]{:S(2)}, u32[]{:S(2)}) collective-permute-start(bf16[1024,128]{1,0:T(8,128)(2,1)S(1)} %get-tuple-element.19), channel_id=1, source_target_pairs={{0,64},{1,193},{2,66},{3,195},{4,68},{5,197},{6,70},{7,199},{8,72}... | collective-permute-start | bytes 786440 | tf_op jit(solution)/shard_map/ppermute | solution.py:237
  3.4 15.1 %collective-permute-start.1 = (bf16[1024,128]{1,0:T(8,128)(2,1)S(1)}, bf16[1024,128]{1,0:T(8,128)(2,1)S(1)}, u32[]{:S(2)}, u32[]{:S(2)}) collective-permute-start(bf16[1024,128]{1,0:T(8,128)(2,1)S(1)} %get-tuple-element.20), channel_id=1, source_target_pairs={{0,128},{1,129},{2,130},{3,131},{4,132},{5,133},{6,134},{7,135},{8... | collective-permute-start | bytes 786440 | tf_op jit(solution)/shard_map/ppermute | solution.py:237
  6.3 6.8 %copy-start.1 = (bf16[2048,128]{1,0:T(8,128)(2,1)S(1)}, bf16[2048,128]{1,0:T(8,128)(2,1)}, u32[]{:S(2)}) copy-start(bf16[2048,128]{1,0:T(8,128)(2,1)} %press_hbm.1) | copy-start | bytes 1572868
  6.3 6.8 %copy-start.2 = (bf16[512,256]{1,0:T(8,128)(2,1)S(1)}, bf16[512,256]{1,0:T(8,128)(2,1)}, u32[]{:S(2)}) copy-start(bf16[512,256]{1,0:T(8,128)(2,1)} %comb_hbm.1) | copy-start | bytes 786436
  6.3 6.8 %copy-start.3 = (s32[2048,1]{0,1:T(1,128)S(1)}, s32[2048,1]{0,1:T(1,128)}, u32[]{:S(2)}) copy-start(s32[2048,1]{0,1:T(1,128)} %param.8) | copy-start | bytes 24580
  6.3 6.8 %copy-start.4 = (s32[2048]{0:T(1024)S(1)}, s32[2048]{0:T(1024)}, u32[]{:S(2)}) copy-start(s32[2048]{0:T(1024)} %param.9) | copy-start | bytes 24580
  6.4 12.2 %collective-permute-start.2 = (bf16[1024,128]{1,0:T(8,128)(2,1)S(1)}, bf16[1024,128]{1,0:T(8,128)(2,1)S(1)}, u32[]{:S(2)}, u32[]{:S(2)}) collective-permute-start(bf16[1024,128]{1,0:T(8,128)(2,1)S(1)} %get-tuple-element.21), channel_id=1, source_target_pairs={{0,192},{1,65},{2,194},{3,67},{4,196},{5,69},{6,198},{7,71},{8,200... | collective-permute-start | bytes 786440 | tf_op jit(solution)/shard_map/ppermute | solution.py:237
  19.3 1.6 %collective-permute-start.3 = (bf16[1056,128]{1,0:T(8,128)(2,1)S(1)}, bf16[1056,128]{1,0:T(8,128)(2,1)S(1)}, u32[]{:S(2)}, u32[]{:S(2)}) collective-permute-start(bf16[1056,128]{1,0:T(8,128)(2,1)S(1)} %get-tuple-element.29), channel_id=1, source_target_pairs={{0,1},{1,0},{2,3},{3,2},{4,5},{5,4},{6,7},{7,6},{8,9},{9,8},{10,11... | collective-permute-start | bytes 811016 | tf_op jit(solution)/shard_map/ppermute | solution.py:283
  49.8 6.3 %collective-permute-start.4 = (bf16[256,128]{1,0:T(8,128)(2,1)S(1)}, bf16[256,128]{1,0:T(8,128)(2,1)S(1)}, u32[]{:S(2)}, u32[]{:S(2)}) collective-permute-start(bf16[256,128]{1,0:T(8,128)(2,1)S(1)} %scatter.1.refs_0_), channel_id=1, source_target_pairs={{0,64},{1,193},{2,66},{3,195},{4,68},{5,197},{6,70},{7,199},{8,72}... | collective-permute-start | bytes 196616 | tf_op jit(solution)/shard_map/ppermute | solution.py:237
  49.9 6.2 %collective-permute-start.5 = (bf16[256,128]{1,0:T(8,128)(2,1)S(1)}, bf16[256,128]{1,0:T(8,128)(2,1)S(1)}, u32[]{:S(2)}, u32[]{:S(2)}) collective-permute-start(bf16[256,128]{1,0:T(8,128)(2,1)S(1)} %scatter.1.refs_0_), channel_id=1, source_target_pairs={{0,128},{1,129},{2,130},{3,131},{4,132},{5,133},{6,134},{7,135},{8... | collective-permute-start | bytes 196616 | tf_op jit(solution)/shard_map/ppermute | solution.py:237
  52.6 4.3 %collective-permute-start.6 = (bf16[256,128]{1,0:T(8,128)(2,1)S(1)}, bf16[256,128]{1,0:T(8,128)(2,1)S(1)}, u32[]{:S(2)}, u32[]{:S(2)}) collective-permute-start(bf16[256,128]{1,0:T(8,128)(2,1)S(1)} %scatter.1.refs_0_), channel_id=1, source_target_pairs={{0,192},{1,65},{2,194},{3,67},{4,196},{5,69},{6,198},{7,71},{8,200... | collective-permute-start | bytes 196616 | tf_op jit(solution)/shard_map/ppermute | solution.py:237
